TPU v7x, 512 devices: a whole 4x8x8 slice. The times are simulated.
512 devices in a mesh: depth: 32 (over x, y), image: 16 (over z, core).
Axes of the slice: x: 4, y: 8, z: 8, core: 2. Of those that a mesh axis runs over, the one named last changes fastest.
Arguments:
- bricks: bfloat16 [32, 4096, 16, 256], P('depth', 'image'), may hold values from -6 to 6
- cost: int32 [32, 4096], P('depth', 'image'), may hold values from 0 to 4, as said below
- order: int32 [2, 32], replicated, may hold values from 0 to 31, as said below
- color_gain: float32 [3], replicated, may hold values from 0.5 to 2
- color_bias: float32 [3], replicated, may hold values from -1 to 1
- ext_gain: float32 [1], replicated, may hold values from 0.6 to 1.4
- ext_bias: float32 [1], replicated, may hold values from -4.6 to -3.6
Outputs:
- frames: float32 [2, 4, 256, 4096], P(None, None, 'depth', 'image')
Inputs may be any that keep to these rules, and one draw needn't show every extreme that they name: In each slab the 16 tiles hold together exactly 2048 bricks of cost above 0, and one tile of each slab has all 256 of its bricks nonempty. `order`: row v holds, for slab s, the bitwise exclusive or of s with a number m_v of 0 to 32 - 1 (the same for the whole row).
All inputs are finite; a program needn't handle non-finite values.
Results may differ from a plain program's by a relative error of at most 0.0003.
Values may be sent and summed in bfloat16 or wider, within the bound.
A program may use at most 128 MiB of HBM per device.

v0:
```python
import math

import jax
import jax.numpy as jnp
from jax import lax
from jax.sharding import PartitionSpec as P

BC = 16


SHEAR = (0.45, -0.3)


def shear_taps(brick_edge, view):
    slice_index = jnp.arange(brick_edge, dtype=jnp.float32)[:, None]
    position = jnp.arange(brick_edge, dtype=jnp.float32)[None, :] + SHEAR[view] * (
        slice_index - (brick_edge - 1) / 2.0
    )
    anchor = jnp.floor(position)
    fraction = position - anchor
    weight_low = lax.optimization_barrier((1.0 - fraction).astype(jnp.bfloat16)).astype(jnp.float32)
    weight_high = lax.optimization_barrier(fraction.astype(jnp.bfloat16)).astype(jnp.float32)
    return (anchor.astype(jnp.int32), weight_low, weight_high)


def shear_table(brick_edge):
    cells = jnp.arange(brick_edge * brick_edge, dtype=jnp.int32)
    source_row = (cells // brick_edge)[None, :, None]
    source_col = (cells % brick_edge)[None, :, None]
    target_row = (cells // brick_edge)[None, None, :]
    target_col = (cells % brick_edge)[None, None, :]
    tables = []
    for view in range(2):
        anchor, weight_low, weight_high = shear_taps(brick_edge, view)
        if view == 0:
            along_target = cells % brick_edge
            same_line = source_row == target_row
            moving = source_col
        else:
            along_target = cells // brick_edge
            same_line = source_col == target_col
            moving = source_row
        start_cell = anchor[:, along_target][:, None, :]
        entry = jnp.where(
            same_line & (moving == start_cell), weight_low[:, along_target][:, None, :], 0.0
        )
        entry = entry + jnp.where(
            same_line & (moving == start_cell + 1), weight_high[:, along_target][:, None, :], 0.0
        )
        tables.append(entry.astype(jnp.bfloat16))
    return jnp.stack(tables)


def shade_samples(samples, levels, flip, color_gain, color_bias, ext_gain, ext_bias):
    brick_edge = samples.shape[1]
    slice_index = jnp.arange(brick_edge, dtype=jnp.int32)
    occupied = (slice_index[None, :] * 4 < levels[:, None] * brick_edge).astype(samples.dtype)[
        :, :, None
    ]
    samples = jnp.where(flip, samples[:, ::-1], samples)
    occupied = jnp.where(flip, occupied[:, ::-1], occupied)
    extinction = jnp.exp(ext_gain[0] * samples + ext_bias[0])
    opacity = (1.0 - jnp.exp(-extinction)) * occupied
    remaining = jnp.cumprod(1.0 - opacity, axis=1)
    ahead_clear = jnp.concatenate([jnp.ones_like(remaining[:, :1]), remaining[:, :-1]], axis=1)
    weight = ahead_clear * opacity
    colors = [
        jnp.sum(
            weight * jax.nn.sigmoid(color_gain[channel] * samples + color_bias[channel]), axis=1
        )
        for channel in range(3)
    ]
    return jnp.stack(colors + [1.0 - remaining[:, -1]], axis=1)


def render(density, levels, table, flips, transfer):
    total_bricks = density.shape[0]
    block_size = math.gcd(total_bricks, 32)

    def render_block(pair):
        block_density, block_levels = pair
        views = []
        for view in range(2):
            samples = jnp.einsum(
                "nkp,kpq->nkq", block_density, table[view], preferred_element_type=jnp.float32
            )
            views.append(shade_samples(samples, block_levels, flips[view], *transfer))
        return jnp.stack(views, axis=1)

    blocks = (
        density.reshape(total_bricks // block_size, block_size, density.shape[1], density.shape[2]),
        levels.reshape(total_bricks // block_size, block_size),
    )
    rendered = lax.map(render_block, blocks)
    return rendered.reshape(total_bricks, 2, 4, density.shape[2])


def composite(front_part, back_part):
    return front_part + (1.0 - front_part[..., 3:4, :, :]) * back_part


def shards(bricks, cost, order, color_gain, color_bias, ext_gain, ext_bias):
    density = bricks[0]
    levels = cost[0]
    brick_count, brick_edge, plane_size = density.shape
    flips = order[:, 0] > order[:, -1]
    masks = order[:, 0]
    table = shear_table(brick_edge)
    transfer = (color_gain, color_bias, ext_gain, ext_bias)
    segments = render(density, levels, table, flips, transfer)
    rows = brick_count // BC
    tile_image = segments.reshape(rows, BC, 2, 4, brick_edge, brick_edge).transpose(
        2, 3, 0, 4, 1, 5
    )
    tile_image = tile_image.reshape(2, 4, rows * brick_edge, BC * brick_edge)
    depth_count = lax.axis_size("depth")
    stacked = lax.all_to_all(tile_image[None], "depth", split_axis=3, concat_axis=0, tiled=True)
    slab_numbers = jnp.arange(depth_count, dtype=jnp.int32)
    views = []
    for view in range(2):
        ranked_slabs = jnp.bitwise_xor(slab_numbers, masks[view])
        views.append(stacked[ranked_slabs, view])
    ordered = jnp.stack(views, axis=1)
    while ordered.shape[0] > 1:
        ordered = composite(ordered[0::2], ordered[1::2])
    return ordered[0]


def solution(mesh):
    in_specs = (P("depth", "image", None, None), P("depth", "image"), P(), P(), P(), P(), P())
    out_specs = P(None, None, "depth", "image")
    return jax.shard_map(shards, mesh=mesh, in_specs=in_specs, out_specs=out_specs, check_vma=False)
```

profile of v0, /device:TPU:336, one launch (start us, length us, event | category | flops | bytes accessed | tf_op | source)
XLA Modules:
  0.0 297.9 jit_solution(4137951500845943421)
XLA Ops:
  6.9 184.8 %while.11 = (s32[]{:T(128)}, f32[8,32,2,4,256]{4,1,0,3,2:T(8,128)S(1)}, f32[1]{0:T(128)}, pred[2]{0:T(512)(128)(4,1)S(1)}, bf16[8,32,16,256]{3,2,1,0:T(8,128)(2,...) while((s32[]{:T(128)}, ...), condition=%wide.region_9.10_spmd.clone, body=%wide.region_0.9_spmd.clone.sunk | while | flops 164334640 | bytes 11951123 | solution.py:94
  7.6 1.3 fusion.67
  8.9 1.0 constant_dynamic-slice_fusion.3
  9.9 1.8 fusion.64
  11.7 1.8 fusion.68
  13.5 2.9 subtract_multiply_fusion.3
  17.2 6.3 %multiply_reduce_fusion.9 = (f32[32,256]{1,0:T(8,128)S(1)}, f32[32,256]{1,0:T(8,128)S(1)}, f32[32,256]{1,0:T(8,128)S(1)}) fusion(f32[32,16,256]{2,0,1:T(8,128)S(1)} %fusion.68, f32[]{:T(128)} %bitcast.118, f32[]{:T(128)} %bitcast.119, pred[]{:T(512)} %bitcast.114, f32[32,15,256]{2,0,1:T(8,128)S(1)} %slice.225, f32[32,16]{0,1:T(8,128)S(1)} %get-tuple-element.446, ...), kind=kLoop, calls=%fused_computation.31.clone.1 | loop fusion | flops 3645440 | bytes 1116193 | tf_op jit(solution)/shard_map/while/body/eval_jaxpr/reduce_sum | solution.py:68
  23.7 6.2 %multiply_reduce_fusion.8 = (f32[32,256]{1,0:T(8,128)S(1)}, f32[32,256]{1,0:T(8,128)S(1)}, f32[32,256]{1,0:T(8,128)S(1)}) fusion(f32[32,16,256]{2,0,1:T(8,128)S(1)} %fusion.64, f32[]{:T(128)} %bitcast.118, f32[]{:T(128)} %bitcast.119, pred[]{:T(512)} %bitcast.115, f32[32,15,256]{2,0,1:T(8,128)S(1)} %slice.224, f32[32,16]{0,1:T(8,128)S(1)} %get-tuple-element.445, ...), kind=kLoop, calls=%fused_computation.24.clone.1 | loop fusion | flops 3645440 | bytes 1116193 | tf_op jit(solution)/shard_map/while/body/eval_jaxpr/reduce_sum | solution.py:68
  30.7 1.3 fusion.67
  32.0 1.0 constant_dynamic-slice_fusion.3
  33.0 1.8 fusion.64
  34.8 1.8 fusion.68
  36.6 2.9 subtract_multiply_fusion.3
  40.3 6.3 %multiply_reduce_fusion.9 = (f32[32,256]{1,0:T(8,128)S(1)}, f32[32,256]{1,0:T(8,128)S(1)}, f32[32,256]{1,0:T(8,128)S(1)}) fusion(f32[32,16,256]{2,0,1:T(8,128)S(1)} %fusion.68, f32[]{:T(128)} %bitcast.118, f32[]{:T(128)} %bitcast.119, pred[]{:T(512)} %bitcast.114, f32[32,15,256]{2,0,1:T(8,128)S(1)} %slice.225, f32[32,16]{0,1:T(8,128)S(1)} %get-tuple-element.446, ...), kind=kLoop, calls=%fused_computation.31.clone.1 | loop fusion | flops 3645440 | bytes 1116193 | tf_op jit(solution)/shard_map/while/body/eval_jaxpr/reduce_sum | solution.py:68
  46.8 6.2 %multiply_reduce_fusion.8 = (f32[32,256]{1,0:T(8,128)S(1)}, f32[32,256]{1,0:T(8,128)S(1)}, f32[32,256]{1,0:T(8,128)S(1)}) fusion(f32[32,16,256]{2,0,1:T(8,128)S(1)} %fusion.64, f32[]{:T(128)} %bitcast.118, f32[]{:T(128)} %bitcast.119, pred[]{:T(512)} %bitcast.115, f32[32,15,256]{2,0,1:T(8,128)S(1)} %slice.224, f32[32,16]{0,1:T(8,128)S(1)} %get-tuple-element.445, ...), kind=kLoop, calls=%fused_computation.24.clone.1 | loop fusion | flops 3645440 | bytes 1116193 | tf_op jit(solution)/shard_map/while/body/eval_jaxpr/reduce_sum | solution.py:68
  53.8 1.3 fusion.67
  55.1 1.0 constant_dynamic-slice_fusion.3
  56.1 1.8 fusion.64
  57.9 1.8 fusion.68
  59.7 2.9 subtract_multiply_fusion.3
  63.4 6.3 %multiply_reduce_fusion.9 = (f32[32,256]{1,0:T(8,128)S(1)}, f32[32,256]{1,0:T(8,128)S(1)}, f32[32,256]{1,0:T(8,128)S(1)}) fusion(f32[32,16,256]{2,0,1:T(8,128)S(1)} %fusion.68, f32[]{:T(128)} %bitcast.118, f32[]{:T(128)} %bitcast.119, pred[]{:T(512)} %bitcast.114, f32[32,15,256]{2,0,1:T(8,128)S(1)} %slice.225, f32[32,16]{0,1:T(8,128)S(1)} %get-tuple-element.446, ...), kind=kLoop, calls=%fused_computation.31.clone.1 | loop fusion | flops 3645440 | bytes 1116193 | tf_op jit(solution)/shard_map/while/body/eval_jaxpr/reduce_sum | solution.py:68
  69.9 6.2 %multiply_reduce_fusion.8 = (f32[32,256]{1,0:T(8,128)S(1)}, f32[32,256]{1,0:T(8,128)S(1)}, f32[32,256]{1,0:T(8,128)S(1)}) fusion(f32[32,16,256]{2,0,1:T(8,128)S(1)} %fusion.64, f32[]{:T(128)} %bitcast.118, f32[]{:T(128)} %bitcast.119, pred[]{:T(512)} %bitcast.115, f32[32,15,256]{2,0,1:T(8,128)S(1)} %slice.224, f32[32,16]{0,1:T(8,128)S(1)} %get-tuple-element.445, ...), kind=kLoop, calls=%fused_computation.24.clone.1 | loop fusion | flops 3645440 | bytes 1116193 | tf_op jit(solution)/shard_map/while/body/eval_jaxpr/reduce_sum | solution.py:68
  76.9 1.3 fusion.67
  79.2 1.8 fusion.64
  81.0 1.8 fusion.68
  82.8 2.9 subtract_multiply_fusion.3
  86.5 6.3 %multiply_reduce_fusion.9 = (f32[32,256]{1,0:T(8,128)S(1)}, f32[32,256]{1,0:T(8,128)S(1)}, f32[32,256]{1,0:T(8,128)S(1)}) fusion(f32[32,16,256]{2,0,1:T(8,128)S(1)} %fusion.68, f32[]{:T(128)} %bitcast.118, f32[]{:T(128)} %bitcast.119, pred[]{:T(512)} %bitcast.114, f32[32,15,256]{2,0,1:T(8,128)S(1)} %slice.225, f32[32,16]{0,1:T(8,128)S(1)} %get-tuple-element.446, ...), kind=kLoop, calls=%fused_computation.31.clone.1 | loop fusion | flops 3645440 | bytes 1116193 | tf_op jit(solution)/shard_map/while/body/eval_jaxpr/reduce_sum | solution.py:68
  93.0 6.2 %multiply_reduce_fusion.8 = (f32[32,256]{1,0:T(8,128)S(1)}, f32[32,256]{1,0:T(8,128)S(1)}, f32[32,256]{1,0:T(8,128)S(1)}) fusion(f32[32,16,256]{2,0,1:T(8,128)S(1)} %fusion.64, f32[]{:T(128)} %bitcast.118, f32[]{:T(128)} %bitcast.119, pred[]{:T(512)} %bitcast.115, f32[32,15,256]{2,0,1:T(8,128)S(1)} %slice.224, f32[32,16]{0,1:T(8,128)S(1)} %get-tuple-element.445, ...), kind=kLoop, calls=%fused_computation.24.clone.1 | loop fusion | flops 3645440 | bytes 1116193 | tf_op jit(solution)/shard_map/while/body/eval_jaxpr/reduce_sum | solution.py:68
  100.0 1.3 fusion.67
  101.3 1.0 constant_dynamic-slice_fusion.3
  102.3 1.8 fusion.64
  104.1 1.8 fusion.68
  105.9 2.9 subtract_multiply_fusion.3
  109.6 6.3 %multiply_reduce_fusion.9 = (f32[32,256]{1,0:T(8,128)S(1)}, f32[32,256]{1,0:T(8,128)S(1)}, f32[32,256]{1,0:T(8,128)S(1)}) fusion(f32[32,16,256]{2,0,1:T(8,128)S(1)} %fusion.68, f32[]{:T(128)} %bitcast.118, f32[]{:T(128)} %bitcast.119, pred[]{:T(512)} %bitcast.114, f32[32,15,256]{2,0,1:T(8,128)S(1)} %slice.225, f32[32,16]{0,1:T(8,128)S(1)} %get-tuple-element.446, ...), kind=kLoop, calls=%fused_computation.31.clone.1 | loop fusion | flops 3645440 | bytes 1116193 | tf_op jit(solution)/shard_map/while/body/eval_jaxpr/reduce_sum | solution.py:68
  116.1 6.2 %multiply_reduce_fusion.8 = (f32[32,256]{1,0:T(8,128)S(1)}, f32[32,256]{1,0:T(8,128)S(1)}, f32[32,256]{1,0:T(8,128)S(1)}) fusion(f32[32,16,256]{2,0,1:T(8,128)S(1)} %fusion.64, f32[]{:T(128)} %bitcast.118, f32[]{:T(128)} %bitcast.119, pred[]{:T(512)} %bitcast.115, f32[32,15,256]{2,0,1:T(8,128)S(1)} %slice.224, f32[32,16]{0,1:T(8,128)S(1)} %get-tuple-element.445, ...), kind=kLoop, calls=%fused_computation.24.clone.1 | loop fusion | flops 3645440 | bytes 1116193 | tf_op jit(solution)/shard_map/while/body/eval_jaxpr/reduce_sum | solution.py:68
  123.1 1.3 fusion.67
  124.4 1.0 constant_dynamic-slice_fusion.3
  125.4 1.8 fusion.64
  127.2 1.8 fusion.68
  129.0 2.9 subtract_multiply_fusion.3
  132.7 6.3 %multiply_reduce_fusion.9 = (f32[32,256]{1,0:T(8,128)S(1)}, f32[32,256]{1,0:T(8,128)S(1)}, f32[32,256]{1,0:T(8,128)S(1)}) fusion(f32[32,16,256]{2,0,1:T(8,128)S(1)} %fusion.68, f32[]{:T(128)} %bitcast.118, f32[]{:T(128)} %bitcast.119, pred[]{:T(512)} %bitcast.114, f32[32,15,256]{2,0,1:T(8,128)S(1)} %slice.225, f32[32,16]{0,1:T(8,128)S(1)} %get-tuple-element.446, ...), kind=kLoop, calls=%fused_computation.31.clone.1 | loop fusion | flops 3645440 | bytes 1116193 | tf_op jit(solution)/shard_map/while/body/eval_jaxpr/reduce_sum | solution.py:68
  139.2 6.2 %multiply_reduce_fusion.8 = (f32[32,256]{1,0:T(8,128)S(1)}, f32[32,256]{1,0:T(8,128)S(1)}, f32[32,256]{1,0:T(8,128)S(1)}) fusion(f32[32,16,256]{2,0,1:T(8,128)S(1)} %fusion.64, f32[]{:T(128)} %bitcast.118, f32[]{:T(128)} %bitcast.119, pred[]{:T(512)} %bitcast.115, f32[32,15,256]{2,0,1:T(8,128)S(1)} %slice.224, f32[32,16]{0,1:T(8,128)S(1)} %get-tuple-element.445, ...), kind=kLoop, calls=%fused_computation.24.clone.1 | loop fusion | flops 3645440 | bytes 1116193 | tf_op jit(solution)/shard_map/while/body/eval_jaxpr/reduce_sum | solution.py:68
  146.2 1.3 fusion.67
  148.5 1.8 fusion.64
  150.3 1.8 fusion.68
  152.1 2.9 subtract_multiply_fusion.3
  155.8 6.3 %multiply_reduce_fusion.9 = (f32[32,256]{1,0:T(8,128)S(1)}, f32[32,256]{1,0:T(8,128)S(1)}, f32[32,256]{1,0:T(8,128)S(1)}) fusion(f32[32,16,256]{2,0,1:T(8,128)S(1)} %fusion.68, f32[]{:T(128)} %bitcast.118, f32[]{:T(128)} %bitcast.119, pred[]{:T(512)} %bitcast.114, f32[32,15,256]{2,0,1:T(8,128)S(1)} %slice.225, f32[32,16]{0,1:T(8,128)S(1)} %get-tuple-element.446, ...), kind=kLoop, calls=%fused_computation.31.clone.1 | loop fusion | flops 3645440 | bytes 1116193 | tf_op jit(solution)/shard_map/while/body/eval_jaxpr/reduce_sum | solution.py:68
  162.3 6.2 %multiply_reduce_fusion.8 = (f32[32,256]{1,0:T(8,128)S(1)}, f32[32,256]{1,0:T(8,128)S(1)}, f32[32,256]{1,0:T(8,128)S(1)}) fusion(f32[32,16,256]{2,0,1:T(8,128)S(1)} %fusion.64, f32[]{:T(128)} %bitcast.118, f32[]{:T(128)} %bitcast.119, pred[]{:T(512)} %bitcast.115, f32[32,15,256]{2,0,1:T(8,128)S(1)} %slice.224, f32[32,16]{0,1:T(8,128)S(1)} %get-tuple-element.445, ...), kind=kLoop, calls=%fused_computation.24.clone.1 | loop fusion | flops 3645440 | bytes 1116193 | tf_op jit(solution)/shard_map/while/body/eval_jaxpr/reduce_sum | solution.py:68
  169.3 1.3 fusion.67
  170.6 1.0 constant_dynamic-slice_fusion.3
  171.6 1.8 fusion.64
  173.4 1.8 fusion.68
  175.2 2.9 subtract_multiply_fusion.3
  178.9 6.3 %multiply_reduce_fusion.9 = (f32[32,256]{1,0:T(8,128)S(1)}, f32[32,256]{1,0:T(8,128)S(1)}, f32[32,256]{1,0:T(8,128)S(1)}) fusion(f32[32,16,256]{2,0,1:T(8,128)S(1)} %fusion.68, f32[]{:T(128)} %bitcast.118, f32[]{:T(128)} %bitcast.119, pred[]{:T(512)} %bitcast.114, f32[32,15,256]{2,0,1:T(8,128)S(1)} %slice.225, f32[32,16]{0,1:T(8,128)S(1)} %get-tuple-element.446, ...), kind=kLoop, calls=%fused_computation.31.clone.1 | loop fusion | flops 3645440 | bytes 1116193 | tf_op jit(solution)/shard_map/while/body/eval_jaxpr/reduce_sum | solution.py:68
  185.4 6.2 %multiply_reduce_fusion.8 = (f32[32,256]{1,0:T(8,128)S(1)}, f32[32,256]{1,0:T(8,128)S(1)}, f32[32,256]{1,0:T(8,128)S(1)}) fusion(f32[32,16,256]{2,0,1:T(8,128)S(1)} %fusion.64, f32[]{:T(128)} %bitcast.118, f32[]{:T(128)} %bitcast.119, pred[]{:T(512)} %bitcast.115, f32[32,15,256]{2,0,1:T(8,128)S(1)} %slice.224, f32[32,16]{0,1:T(8,128)S(1)} %get-tuple-element.445, ...), kind=kLoop, calls=%fused_computation.24.clone.1 | loop fusion | flops 3645440 | bytes 1116193 | tf_op jit(solution)/shard_map/while/body/eval_jaxpr/reduce_sum | solution.py:68
  191.7 8.6 %reshape_reshape.3 = f32[16,16,2,4,16,16]{5,4,1,0,3,2:T(8,128)} reshape(f32[8,32,2,4,256]{4,1,0,3,2:T(8,128)S(1)} %get-tuple-element.62) | data formatting | bytes 4194304 | tf_op jit(solution)/shard_map/reshape;reshape | solution.py:112
  200.3 15.8 %copy.65 = f32[2,4,16,16,16,16]{5,4,1,0,3,2:T(8,128)} copy(f32[2,4,16,16,16,16]{5,3,4,2,1,0:T(8,128)} %bitcast.130) | data formatting | bytes 4194304 | tf_op jit(solution)/shard_map/broadcast_in_dim;reshape | solution.py:117
  216.2 12.7 %reshape.293 = f32[1,2,4,256,256]{4,2,1,0,3:T(4,128)} reshape(f32[2,4,16,16,16,16]{5,4,1,0,3,2:T(8,128)} %copy.65) | data formatting | bytes 4194304 | tf_op jit(solution)/shard_map/broadcast_in_dim;reshape | solution.py:117
  228.9 10.1 %all-to-all-start = ((f32[1,2,4,256,256]{4,2,1,0,3:T(4,128)}), f32[1,2,4,256,256]{4,2,1,0,3:T(4,128)S(1)}, u32[]{:S(2)}, u32[]{:S(2)}) async-start(f32[1,2,4,256,256]{4,2,1,0,3:T(4,128)} %reshape.293), calls=%async_computation | async-start | bytes 4194304 | tf_op jit(solution)/shard_map/all_to_all | solution.py:117
  240.9 48.1 %all-to-all-done = f32[1,2,4,256,256]{4,2,1,0,3:T(4,128)S(1)} async-done(((f32[1,2,4,256,256]{4,2,1,0,3:T(4,128)}), f32[1,2,4,256,256]{4,2,1,0,3:T(4,128)S(1)}, u32[]{:S(2)}, u32[]{:S(2)}) %all-to-all-start) | async-done | bytes 2097184 | tf_op jit(solution)/shard_map/all_to_all | solution.py:117
  289.0 2.2 copy.76
  291.2 2.4 gather_fusion.6
  293.6 1.6 gather_fusion.7
  295.2 1.4 pad_maximum_fusion
  (185 shorter events, 25.4 us)
Async XLA Ops:
  0.0 5.7 %copy-start.4 = (s32[1,256]{1,0:T(1,128)S(1)}, s32[1,256]{1,0:T(1,128)}, u32[]{:S(2)}) copy-start(s32[1,256]{1,0:T(1,128)} %param.10) | copy-start | bytes 3076
  0.0 6.5 %copy-start.3 = (s32[2,32]{1,0:T(2,128)S(1)}, s32[2,32]{1,0:T(2,128)}, u32[]{:S(2)}) copy-start(s32[2,32]{1,0:T(2,128)} %param.11) | copy-start | bytes 772
  0.0 6.9 %copy-start.1 = (f32[3]{0:T(128)S(1)}, f32[3]{0:T(128)}, u32[]{:S(2)}) copy-start(f32[3]{0:T(128)} %param.12) | copy-start | bytes 40
  0.0 6.9 %copy-start.2 = (f32[3]{0:T(128)S(1)}, f32[3]{0:T(128)}, u32[]{:S(2)}) copy-start(f32[3]{0:T(128)} %param.13) | copy-start | bytes 40
  228.9 60.1 %all-to-all-start = ((f32[1,2,4,256,256]{4,2,1,0,3:T(4,128)}), f32[1,2,4,256,256]{4,2,1,0,3:T(4,128)S(1)}, u32[]{:S(2)}, u32[]{:S(2)}) async-start(f32[1,2,4,256,256]{4,2,1,0,3:T(4,128)} %reshape.293), calls=%async_computation | async-start | bytes 4194304 | tf_op jit(solution)/shard_map/all_to_all | solution.py:117
  291.2 2.4 copy-start
where the time goes:
time: 300 us; the launch traced here: 298 us
  other arithmetic  141 us (47%)
  local copies, waits for them, and re-layouts  68.4 us (23%)
  waiting for transfers between devices  48.1 us (16%)
  matrix products  28.7 us (10%)
  starting transfers between devices  10.1 us (3%)
    reduce_sum x16, other arithmetic, shade_samples(): jnp.sum(weight * jax.nn.sigmoid(color_gain[channel] * samples + color_bia...  100 us
    all_to_all x1, waiting for transfers between devices, shards(): lax.all_to_all(tile_image[None], 'depth', split_axis=3, concat_axis=0, ti...  48.1 us
    dot_general x16, matrix products, render_block(): jnp.einsum('nkp,kpq->nkq', block_density, table[view], preferred_element_...  28.7 us
    another operation x2, local copies, waits for them, and re-layouts, shards(): tile_image[None]  28.5 us
    mul x8, other arithmetic, shade_samples(): opacity = (1.0 - jnp.exp(-extinction)) * occupied  23 us
    select_n x8, other arithmetic, shade_samples(): occupied = jnp.where(flip, occupied[:, ::-1], occupied)  10.5 us
    all_to_all x1, starting transfers between devices, shards(): lax.all_to_all(tile_image[None], 'depth', split_axis=3, concat_axis=0, ti...  10.1 us
    another operation x1, local copies, waits for them, and re-layouts, shards(): segments.reshape(rows, BC, 2, 4, brick_edge, brick_edge)  8.64 us
  transfers between devices with their start and end apart: 1, of which 1 were waited for; matrix products, arithmetic and copies ran while one was open for 1% of the time, Pallas kernels for 0%

commit v1 on v0

v1 whole, which is shorter than its diff:
```python
import jax
import jax.numpy as jnp
import numpy as np
import ml_dtypes
from jax import lax
from jax.experimental import pallas as pl
from jax.experimental.pallas import tpu as pltpu
from jax.sharding import PartitionSpec as P

BE = 16
PX = BE * BE
NB = 256
NX = 4
NY = 8
CHUNK = NB // NX
SHEAR = (0.45, -0.3)
LOG2E = 1.4426950408889634
TOP = 65535.0
MESH = pl.DeviceIdType.MESH


def shear_table():
    cells = np.arange(PX)
    rows, cols = cells // BE, cells % BE
    out = np.zeros((2, BE, PX, PX), np.float32)
    for view in range(2):
        k = np.arange(BE, dtype=np.float32)[:, None]
        position = np.arange(BE, dtype=np.float32)[None, :] + np.float32(SHEAR[view]) * (
            k - np.float32((BE - 1) / 2.0)
        )
        anchor = np.floor(position)
        fraction = (position - anchor).astype(np.float32)
        low = (np.float32(1.0) - fraction).astype(ml_dtypes.bfloat16).astype(np.float32)
        high = fraction.astype(ml_dtypes.bfloat16).astype(np.float32)
        anchor = anchor.astype(np.int32)
        along = cols if view == 0 else rows
        for tap, weight in ((0, low), (1, high)):
            source = anchor[:, along] + tap
            inside = (source >= 0) & (source < BE)
            for s in range(BE):
                index = (rows * BE + source[s]) if view == 0 else (source[s] * BE + cols)
                ok = inside[s]
                out[view, s, index[ok], cells[ok]] += weight[s, along][ok]
    return out.astype(ml_dtypes.bfloat16)


def encode(value):
    root = jnp.exp2(0.25 * jnp.log2(jnp.maximum(value, 1e-30)))
    code = jnp.minimum(root * TOP + 0.5, TOP).astype(jnp.int32) - 32768
    return code.astype(jnp.int16)


def decode(code):
    root = (code.astype(jnp.float32) + 32768.0) * (1.0 / TOP)
    square = root * root
    return square * square


def swap_rows_and_groups(block):
    row = lax.broadcasted_iota(jnp.int32, (8, 128), 0)
    group = lax.broadcasted_iota(jnp.int32, (8, 128), 1) // 16
    for bit in (1, 2, 4):
        row_bit = (row & bit) != 0
        group_bit = (group & bit) != 0
        from_below = pltpu.roll(pltpu.roll(block, 8 - bit, 0), 16 * bit, 1)
        from_above = pltpu.roll(pltpu.roll(block, bit, 0), 128 - 16 * bit, 1)
        moved = jnp.where(row_bit, from_above, from_below)
        block = jnp.where(row_bit == group_bit, block, moved)
    return block


def kernel(
    order, color_gain, color_bias, ext_gain, ext_bias, cost, bricks, table_hbm, out,
    raw, table, sliced, samples, levels, send, recv0, recv1, recv2, recv3, group,
    raw_sem, table_sem, send_sem, recv_sem, own_sem,
):
    me = lax.axis_index("depth")
    x, y = me // NY, me % NY

    def chunk_copy(i):
        c = lax.rem(x + i, NX)
        rows = pl.ds(pl.multiple_of(c * CHUNK * BE, CHUNK * BE), CHUNK * BE)
        return pltpu.make_async_copy(bricks.at[rows], raw.at[i], raw_sem.at[i])

    def table_copy(view):
        return pltpu.make_async_copy(table_hbm.at[view], table.at[view], table_sem.at[view])

    chunk_copy(0).start()
    table_copy(0).start()
    table_copy(1).start()
    for i in range(1, NX):
        chunk_copy(i).start()

    def peer(i, j):
        return lax.rem(x + i, NX) * NY + lax.rem(y + j, NY)

    barrier = pltpu.get_barrier_semaphore()

    def greet(t, carry):
        pl.semaphore_signal(barrier, inc=1, device_id={"depth": lax.rem(me + t, NX * NY)}, device_id_type=MESH)
        return carry

    lax.fori_loop(1, NX * NY, greet, 0)

    r = lax.broadcasted_iota(jnp.int32, (NB, NB), 0)
    q = lax.broadcasted_iota(jnp.int32, (NB, NB), 1)
    diagonal = jnp.where(r == q, (cost[...] * 4).astype(jnp.float32), 0.0).astype(jnp.bfloat16)
    levels[...] = jnp.dot(diagonal, jnp.ones((NB, 128), jnp.bfloat16), preferred_element_type=jnp.float32)
    regroup = jnp.where(q == (r % BE) * BE + r // BE, 1.0, 0.0).astype(jnp.bfloat16)

    masks = [order[v, 0] for v in range(2)]
    turned = [jnp.where(order[v, 0] > order[v, 31], 15, 0) for v in range(2)]
    gain = ext_gain[0] * LOG2E
    bias = ext_bias[0] * LOG2E + float(np.log2(LOG2E))
    half_gain = [color_gain[c] * 0.5 for c in range(3)]
    half_bias = [color_bias[c] * 0.5 for c in range(3)]

    recv = (recv0, recv1, recv2, recv3)

    def remote(i, j):
        slot = i * NY + j
        return pltpu.make_async_remote_copy(
            src_ref=send.at[slot], dst_ref=recv[i].at[j],
            send_sem=send_sem.at[slot], recv_sem=recv_sem.at[slot],
            device_id={"depth": peer(i, j)}, device_id_type=MESH,
        )

    def own_copy():
        return pltpu.make_async_copy(send.at[0], recv0.at[0], own_sem)

    def compute_chunk(i):
        chunk_copy(i).wait()
        for g in range(CHUNK // BE):
            lined = jnp.dot(
                regroup, raw[i, g * PX:(g + 1) * PX, :], preferred_element_type=jnp.float32
            ).astype(jnp.bfloat16)
            for k in range(BE):
                sliced[k, g * BE:(g + 1) * BE, :] = lined[k * BE:(k + 1) * BE, :]

        for view in range(2):
            if isinstance(i, int):
                table_copy(view).wait()

            def resample(k, carry):
                samples[view, k] = jnp.dot(
                    sliced[k], table[view, k], preferred_element_type=jnp.float32
                )
                return carry

            lax.fori_loop(0, BE, resample, 0, unroll=4)

        c = lax.rem(x + i, NX)
        for view in range(2):

            def shade(g, carry):
                rows = pl.ds(pl.multiple_of(g * BE, BE), BE)
                level = levels[pl.ds(pl.multiple_of(c * CHUNK + g * BE, BE), BE), :]
                level = jnp.concatenate([level, level], axis=1)
                depth = jnp.zeros((BE, PX), jnp.float32)
                clear = jnp.ones((BE, PX), jnp.float32)
                tints = [jnp.zeros((BE, PX), jnp.float32) for _ in range(3)]
                for k in range(BE):
                    kk = jnp.bitwise_xor(k, turned[view])
                    s = samples[view, kk, rows, :]
                    b = jnp.where(kk.astype(jnp.float32) < level, bias, -1e9)
                    depth = depth - jnp.exp2(s * gain + b)
                    after = jnp.exp2(depth)
                    weight = clear - after
                    clear = after
                    for ch in range(3):
                        tints[ch] = tints[ch] + weight * jnp.tanh(s * half_gain[ch] + half_bias[ch])
                opaque = 1.0 - clear
                values = [0.5 * (opaque + t) for t in tints] + [opaque]
                for ch in range(4):
                    code = encode(values[ch])
                    for h in range(2):
                        j = lax.rem(2 * g + h - y + NY, NY)
                        send[i * NY + j, view, ch] = code[:, h * 128:(h + 1) * 128]
                return carry

            lax.fori_loop(0, CHUNK // BE, shade, 0)

    def send_chunk(i, first):
        def go(j, carry):
            remote(i, j).start()
            return carry

        lax.fori_loop(first, NY, go, 0)

    compute_chunk(0)
    pl.semaphore_wait(barrier, NX * NY - 1)
    own_copy().start()
    send_chunk(0, 1)

    def later(i, carry):
        compute_chunk(i)
        for step in range(1, NX):
            pl.when(i == step)(lambda step=step: send_chunk(step, 0))
        return carry

    lax.fori_loop(1, NX, later, 0)

    own_copy().wait()
    for i in range(NX):

        def wait_in(j, carry):
            remote(i, j).wait_recv()
            return carry

        lax.fori_loop(1 if i == 0 else 0, NY, wait_in, 0)
        for view in range(2):
            clear = jnp.ones((BE, 128), jnp.float32)
            tints = [jnp.zeros((BE, 128), jnp.float32) for _ in range(3)]
            for rank in range(NY):
                source = jnp.bitwise_xor(rank, masks[view] & (NY - 1))
                j = (y - source) & (NY - 1)
                for ch in range(3):
                    tints[ch] = tints[ch] + clear * decode(recv[i][j, view, ch])
                clear = clear * (1.0 - decode(recv[i][j, view, 3]))
            for ch in range(3):
                group[i, view, ch] = tints[ch]
            group[i, view, 3] = clear

    for view in range(2):
        clear = jnp.ones((BE, 128), jnp.float32)
        tints = [jnp.zeros((BE, 128), jnp.float32) for _ in range(3)]
        for rank in range(NX):
            source = jnp.bitwise_xor(rank, masks[view] // NY)
            i = (x - source) & (NX - 1)
            for ch in range(3):
                tints[ch] = tints[ch] + clear * group[i, view, ch]
            clear = clear * group[i, view, 3]
        for ch, value in enumerate(tints + [1.0 - clear]):
            for h in range(2):
                out[view, ch, :, h * 128:(h + 1) * 128] = swap_rows_and_groups(value[h * 8:(h + 1) * 8, :])

    for i in range(NX):

        def wait_out(j, carry):
            remote(i, j).wait_send()
            return carry

        lax.fori_loop(1 if i == 0 else 0, NY, wait_out, 0)


def shards(bricks, cost, order, color_gain, color_bias, ext_gain, ext_bias):
    table = jnp.asarray(shear_table())
    smem = pl.BlockSpec(memory_space=pltpu.SMEM)
    vmem = pl.BlockSpec(memory_space=pltpu.VMEM)
    anywhere = pl.BlockSpec(memory_space=pl.ANY)
    return pl.pallas_call(
        kernel,
        out_shape=jax.ShapeDtypeStruct((2, 4, 8, 256), jnp.float32),
        in_specs=[smem] * 5 + [vmem, anywhere, anywhere],
        out_specs=vmem,
        scratch_shapes=[
            pltpu.VMEM((NX, CHUNK * BE, PX), jnp.bfloat16),
            pltpu.VMEM((2, BE, PX, PX), jnp.bfloat16),
            pltpu.VMEM((BE, CHUNK, PX), jnp.bfloat16),
            pltpu.VMEM((2, BE, CHUNK, PX), jnp.float32),
            pltpu.VMEM((NB, 128), jnp.float32),
            pltpu.VMEM((NX * NY, 2, 4, BE, 128), jnp.int16),
            *[pltpu.VMEM((NY, 2, 4, BE, 128), jnp.int16) for _ in range(NX)],
            pltpu.VMEM((NX, 2, 4, BE, 128), jnp.float32),
            pltpu.SemaphoreType.DMA((NX,)),
            pltpu.SemaphoreType.DMA((2,)),
            pltpu.SemaphoreType.DMA((NX * NY,)),
            pltpu.SemaphoreType.DMA((NX * NY,)),
            pltpu.SemaphoreType.DMA,
        ],
        compiler_params=pltpu.CompilerParams(
            collective_id=0, has_side_effects=True, vmem_limit_bytes=40 * 2**20
        ),
    )(order, color_gain, color_bias, ext_gain, ext_bias, cost, bricks.reshape(NB * BE, PX), table)


def solution(mesh):
    in_specs = (P("depth", "image", None, None), P("depth", "image"), P(), P(), P(), P(), P())
    out_specs = P(None, None, "depth", "image")
    return jax.shard_map(shards, mesh=mesh, in_specs=in_specs, out_specs=out_specs, check_vma=False)
```

time: 300 us -> 46.1 us (0.15)
  the two profiles are of different devices: /device:TPU:336 before, /device:TPU:450 now
where the time goes in v1:
time: 46.1 us; the launch traced here: 45.8 us
  Pallas kernels  37.5 us (81%)
  local copies, waits for them, and re-layouts  7.07 us (15%)
  between operations  1.32 us (3%)
    pallas_call x1, Pallas kernels, shards(): pl.pallas_call(kernel, out_shape=jax.ShapeDtypeStruct((2, 4, 8, 256), jnp...  37.5 us
    unnamed x13, local copies, waits for them, and re-layouts  7.07 us

profile of v1, /device:TPU:450, one launch (start us, length us, event | category | flops | bytes accessed | tf_op | source)
XLA Modules:
  0.0 45.8 jit_solution(1488636845173840697)
XLA Ops:
  1.3 0.0 copy-start
  1.3 2.2 %copy-done = bf16[2,16,256,256]{3,2,1,0:T(8,128)(2,1)S(1)} copy-done((bf16[2,16,256,256]{3,2,1,0:T(8,128)(2,1)S(1)}, bf16[2,16,256,256]{3,2,1,0:T(8,128)(2,1)}, u32[]{:S(2)}) %copy-start) | copy-done | bytes 4194328
  3.5 0.0 copy-start.1
  3.5 1.6 %copy-done.1 = bf16[1,256,16,256]{3,2,1,0:T(8,128)(2,1)S(1)} copy-done((bf16[1,256,16,256]{3,2,1,0:T(8,128)(2,1)S(1)}, bf16[1,256,16,256]{3,2,1,0:T(8,128)(2,1)}, u32[]{:S(2)}) %copy-start.1) | copy-done | bytes 2097176
  5.1 0.0 copy-start.2
  5.1 0.7 %copy-done.2 = s32[2,32]{1,0:T(2,128)S(1)} copy-done((s32[2,32]{1,0:T(2,128)S(1)}, s32[2,32]{1,0:T(2,128)}, u32[]{:S(2)}) %copy-start.2) | copy-done | bytes 280
  5.8 0.0 copy-start.3
  5.8 0.7 %copy-done.3 = s32[1,256]{1,0:T(1,128)S(1)} copy-done((s32[1,256]{1,0:T(1,128)S(1)}, s32[1,256]{1,0:T(1,128)}, u32[]{:S(2)}) %copy-start.3) | copy-done | bytes 1048
  6.4 0.0 copy-start.4
  6.4 0.7 %copy-done.4 = f32[3]{0:T(128)S(1)} copy-done((f32[3]{0:T(128)S(1)}, f32[3]{0:T(128)}, u32[]{:S(2)}) %copy-start.4) | copy-done | bytes 36
  7.1 0.0 copy-start.5
  7.1 0.7 %copy-done.5 = f32[3]{0:T(128)S(1)} copy-done((f32[3]{0:T(128)S(1)}, f32[3]{0:T(128)}, u32[]{:S(2)}) %copy-start.5) | copy-done | bytes 36
  7.8 37.5 %shard_map.82 = f32[2,4,8,256]{3,2,1,0:T(8,128)S(1)} custom-call(s32[2,32]{1,0:T(2,128)S(1)} %copy-done.2, f32[3]{0:T(128)S(1)} %copy-done.4, f32[3]{0:T(128)S(1)} %copy-done.5, f32[1]{0:T(128)S(6)} %copy.10.ext_gain, f32[1]{0:T(128)S(6)} %copy.11.ext_bias, s32[1,256]{1,0:T(1,128)S(1)} %copy-done.3, bf16[4096,256]{1,0:T(8,128)(2,1)S(1)} %bitcast.1, ...), custom_call_target="tpu_custom_call" | custom-call | tf_op jit(solution)/shard_map/pallas_call | solution.py:251
  45.2 0.6 %copy.12 = f32[2,4,8,256]{3,2,1,0:T(8,128)} copy(f32[2,4,8,256]{3,2,1,0:T(8,128)S(1)} %shard_map.82) | data formatting | bytes 131072
Async XLA Ops:
  1.3 2.2 %copy-start = (bf16[2,16,256,256]{3,2,1,0:T(8,128)(2,1)S(1)}, bf16[2,16,256,256]{3,2,1,0:T(8,128)(2,1)}, u32[]{:S(2)}) copy-start(bf16[2,16,256,256]{3,2,1,0:T(8,128)(2,1)} %constant.2.clone.table_hbm) | copy-start | bytes 12582916
  3.5 1.6 %copy-start.1 = (bf16[1,256,16,256]{3,2,1,0:T(8,128)(2,1)S(1)}, bf16[1,256,16,256]{3,2,1,0:T(8,128)(2,1)}, u32[]{:S(2)}) copy-start(bf16[1,256,16,256]{3,2,1,0:T(8,128)(2,1)} %param.8) | copy-start | bytes 6291460
  5.1 0.7 %copy-start.2 = (s32[2,32]{1,0:T(2,128)S(1)}, s32[2,32]{1,0:T(2,128)}, u32[]{:S(2)}) copy-start(s32[2,32]{1,0:T(2,128)} %order.1) | copy-start | bytes 772
  5.8 0.7 %copy-start.3 = (s32[1,256]{1,0:T(1,128)S(1)}, s32[1,256]{1,0:T(1,128)}, u32[]{:S(2)}) copy-start(s32[1,256]{1,0:T(1,128)} %cost.1) | copy-start | bytes 3076
  6.4 0.7 %copy-start.4 = (f32[3]{0:T(128)S(1)}, f32[3]{0:T(128)}, u32[]{:S(2)}) copy-start(f32[3]{0:T(128)} %color_gain.1) | copy-start | bytes 40
  7.1 0.7 %copy-start.5 = (f32[3]{0:T(128)S(1)}, f32[3]{0:T(128)}, u32[]{:S(2)}) copy-start(f32[3]{0:T(128)} %color_bias.1) | copy-start | bytes 40

commit v2 on v1

--- a/solution.py
+++ b/solution.py
@@ -70,29 +70,43 @@
 
 
 def kernel(
-    order, color_gain, color_bias, ext_gain, ext_bias, cost, bricks, table_hbm, out,
-    raw, table, sliced, samples, levels, send, recv0, recv1, recv2, recv3, group,
-    raw_sem, table_sem, send_sem, recv_sem, own_sem,
+    order_hbm, color_gain_hbm, color_bias_hbm, ext_gain_hbm, ext_bias_hbm, cost_hbm, bricks, table_hbm, out,
+    order, color_gain, color_bias, ext_gain, ext_bias, cost, raw, table, sliced, samples, levels, slab, other, pair_out,
+    pair_in0, pair_in1, pair_in2, pair_in3, group,
+    small_sem, raw_sem, table_sem, slab_send_sem, slab_recv_sem, pair_send_sem, pair_recv_sem, own_sem,
 ):
     me = lax.axis_index("depth")
     x, y = me // NY, me % NY
 
     def chunk_copy(i):
-        c = lax.rem(x + i, NX)
+        c = lax.rem(x + i + 1, NX)
         rows = pl.ds(pl.multiple_of(c * CHUNK * BE, CHUNK * BE), CHUNK * BE)
         return pltpu.make_async_copy(bricks.at[rows], raw.at[i], raw_sem.at[i])
 
     def table_copy(view):
         return pltpu.make_async_copy(table_hbm.at[view], table.at[view], table_sem.at[view])
 
+    small = [
+        pltpu.make_async_copy(source, target, small_sem.at[n])
+        for n, (source, target) in enumerate((
+            (cost_hbm, cost), (order_hbm, order), (ext_gain_hbm, ext_gain), (ext_bias_hbm, ext_bias),
+            (color_gain_hbm, color_gain), (color_bias_hbm, color_bias),
+        ))
+    ]
+    for copy in small:
+        copy.start()
     chunk_copy(0).start()
     table_copy(0).start()
     table_copy(1).start()
     for i in range(1, NX):
         chunk_copy(i).start()
 
-    def peer(i, j):
-        return lax.rem(x + i, NX) * NY + lax.rem(y + j, NY)
+    odd = lax.rem(y, 2)
+    way = 2 * odd - 1
+    partner = x * NY + y - way
+
+    def peer(i, t):
+        return lax.rem(x + i, NX) * NY + lax.rem(y + way * t + NY, NY)
 
     barrier = pltpu.get_barrier_semaphore()
 
@@ -101,6 +115,9 @@
         return carry
 
     lax.fori_loop(1, NX * NY, greet, 0)
+
+    for copy in small:
+        copy.wait()
 
     r = lax.broadcasted_iota(jnp.int32, (NB, NB), 0)
     q = lax.broadcasted_iota(jnp.int32, (NB, NB), 1)
@@ -115,18 +132,24 @@
     half_gain = [color_gain[c] * 0.5 for c in range(3)]
     half_bias = [color_bias[c] * 0.5 for c in range(3)]
 
-    recv = (recv0, recv1, recv2, recv3)
-
-    def remote(i, j):
-        slot = i * NY + j
+    pair_in = (pair_in0, pair_in1, pair_in2, pair_in3)
+
+    def to_partner(n):
         return pltpu.make_async_remote_copy(
-            src_ref=send.at[slot], dst_ref=recv[i].at[j],
-            send_sem=send_sem.at[slot], recv_sem=recv_sem.at[slot],
-            device_id={"depth": peer(i, j)}, device_id_type=MESH,
+            src_ref=slab.at[n, pl.ds(4, 4)], dst_ref=other.at[n],
+            send_sem=slab_send_sem.at[n], recv_sem=slab_recv_sem.at[n],
+            device_id={"depth": partner}, device_id_type=MESH,
         )
 
+    def to_owner(n, t):
+        return pltpu.make_async_remote_copy(
+            src_ref=pair_out.at[n, t], dst_ref=pair_in[n].at[t],
+            send_sem=pair_send_sem.at[n * 4 + t], recv_sem=pair_recv_sem.at[n * 4 + t],
+            device_id={"depth": peer(n + 1, t)}, device_id_type=MESH,
+        )
+
     def own_copy():
-        return pltpu.make_async_copy(send.at[0], recv0.at[0], own_sem)
+        return pltpu.make_async_copy(pair_out.at[NX - 1, 0], pair_in3.at[0], own_sem)
 
     def compute_chunk(i):
         chunk_copy(i).wait()
@@ -149,7 +172,7 @@
 
             lax.fori_loop(0, BE, resample, 0, unroll=4)
 
-        c = lax.rem(x + i, NX)
+        c = lax.rem(x + i + 1, NX)
         for view in range(2):
 
             def shade(g, carry):
@@ -174,102 +197,137 @@
                 for ch in range(4):
                     code = encode(values[ch])
                     for h in range(2):
-                        j = lax.rem(2 * g + h - y + NY, NY)
-                        send[i * NY + j, view, ch] = code[:, h * 128:(h + 1) * 128]
+                        u = lax.rem(way * (2 * g + h - y) + NY, NY)
+                        slab[i, u, view, ch] = code[:, h * 128:(h + 1) * 128]
                 return carry
 
             lax.fori_loop(0, CHUNK // BE, shade, 0)
 
-    def send_chunk(i, first):
-        def go(j, carry):
-            remote(i, j).start()
+    def composite_pair(n):
+        to_partner(n).wait_recv()
+
+        def one(t, carry):
+            for view in range(2):
+                first = (jnp.bitwise_xor(y, masks[view]) & 1) == 0
+                mine = [decode(slab[n, t, view, ch]) for ch in range(4)]
+                theirs = [decode(other[n, 3 - t, view, ch]) for ch in range(4)]
+                keep_mine = jnp.where(first, 1.0, 1.0 - theirs[3])
+                keep_theirs = jnp.where(first, 1.0 - mine[3], 1.0)
+                for ch in range(4):
+                    pair_out[n, t, view, ch] = encode(keep_mine * mine[ch] + keep_theirs * theirs[ch])
             return carry
 
-        lax.fori_loop(first, NY, go, 0)
+        lax.fori_loop(0, 4, one, 0)
+
+    def send_pairs(n):
+        def go(t, carry):
+            to_owner(n, t).start()
+            return carry
+
+        if n == NX - 1:
+            own_copy().start()
+        lax.fori_loop(1 if n == NX - 1 else 0, 4, go, 0)
 
     compute_chunk(0)
     pl.semaphore_wait(barrier, NX * NY - 1)
-    own_copy().start()
-    send_chunk(0, 1)
-
-    def later(i, carry):
-        compute_chunk(i)
-        for step in range(1, NX):
-            pl.when(i == step)(lambda step=step: send_chunk(step, 0))
+    to_partner(0).start()
+
+    def later(n, carry):
+        compute_chunk(n)
+        to_partner(n).start()
+        composite_pair(n - 1)
+        for step in range(NX - 1):
+            pl.when(n - 1 == step)(lambda step=step: send_pairs(step))
         return carry
 
     lax.fori_loop(1, NX, later, 0)
-
-    own_copy().wait()
-    for i in range(NX):
-
-        def wait_in(j, carry):
-            remote(i, j).wait_recv()
+    composite_pair(NX - 1)
+    send_pairs(NX - 1)
+
+    for n in range(NX):
+        first = 0
+        if n == NX - 1:
+            own_copy().wait()
+            first = 1
+
+        def wait_in(t, carry):
+            to_owner(n, t).wait_recv()
             return carry
 
-        lax.fori_loop(1 if i == 0 else 0, NY, wait_in, 0)
+        lax.fori_loop(first, 4, wait_in, 0)
         for view in range(2):
             clear = jnp.ones((BE, 128), jnp.float32)
-            tints = [jnp.zeros((BE, 128), jnp.float32) for _ in range(3)]
-            for rank in range(NY):
-                source = jnp.bitwise_xor(rank, masks[view] & (NY - 1))
-                j = (y - source) & (NY - 1)
-                for ch in range(3):
-                    tints[ch] = tints[ch] + clear * decode(recv[i][j, view, ch])
-                clear = clear * (1.0 - decode(recv[i][j, view, 3]))
-            for ch in range(3):
-                group[i, view, ch] = tints[ch]
-            group[i, view, 3] = clear
+            total = [jnp.zeros((BE, 128), jnp.float32) for _ in range(4)]
+            for rank in range(4):
+                pair = jnp.bitwise_xor(rank, (masks[view] // 2) & 3)
+                delta = (way * (pair - y // 2)) & 3
+                t = jnp.bitwise_xor(delta, delta // 2)
+                for ch in range(4):
+                    total[ch] = total[ch] + clear * decode(pair_in[n][t, view, ch])
+                clear = 1.0 - total[3]
+            for ch in range(4):
+                group[n, view, ch] = total[ch]
 
     for view in range(2):
         clear = jnp.ones((BE, 128), jnp.float32)
-        tints = [jnp.zeros((BE, 128), jnp.float32) for _ in range(3)]
+        total = [jnp.zeros((BE, 128), jnp.float32) for _ in range(4)]
         for rank in range(NX):
             source = jnp.bitwise_xor(rank, masks[view] // NY)
-            i = (x - source) & (NX - 1)
-            for ch in range(3):
-                tints[ch] = tints[ch] + clear * group[i, view, ch]
-            clear = clear * group[i, view, 3]
-        for ch, value in enumerate(tints + [1.0 - clear]):
+            n = (x - source - 1) & (NX - 1)
+            for ch in range(4):
+                total[ch] = total[ch] + clear * group[n, view, ch]
+            clear = 1.0 - total[3]
+        for ch in range(4):
             for h in range(2):
-                out[view, ch, :, h * 128:(h + 1) * 128] = swap_rows_and_groups(value[h * 8:(h + 1) * 8, :])
-
-    for i in range(NX):
-
-        def wait_out(j, carry):
-            remote(i, j).wait_send()
+                out[view, ch, :, h * 128:(h + 1) * 128] = swap_rows_and_groups(total[ch][h * 8:(h + 1) * 8, :])
+
+    for n in range(NX):
+        to_partner(n).wait_send()
+
+        def wait_out(t, carry):
+            to_owner(n, t).wait_send()
             return carry
 
-        lax.fori_loop(1 if i == 0 else 0, NY, wait_out, 0)
+        lax.fori_loop(1 if n == NX - 1 else 0, 4, wait_out, 0)
 
 
 def shards(bricks, cost, order, color_gain, color_bias, ext_gain, ext_bias):
     table = jnp.asarray(shear_table())
-    smem = pl.BlockSpec(memory_space=pltpu.SMEM)
     vmem = pl.BlockSpec(memory_space=pltpu.VMEM)
-    anywhere = pl.BlockSpec(memory_space=pl.ANY)
+    anywhere = pl.BlockSpec(memory_space=pltpu.HBM)
     return pl.pallas_call(
         kernel,
         out_shape=jax.ShapeDtypeStruct((2, 4, 8, 256), jnp.float32),
-        in_specs=[smem] * 5 + [vmem, anywhere, anywhere],
+        in_specs=[anywhere] * 8,
         out_specs=vmem,
         scratch_shapes=[
+            pltpu.SMEM((2, 32), jnp.int32),
+            pltpu.SMEM((3,), jnp.float32),
+            pltpu.SMEM((3,), jnp.float32),
+            pltpu.SMEM((1,), jnp.float32),
+            pltpu.SMEM((1,), jnp.float32),
+            pltpu.VMEM((1, NB), jnp.int32),
             pltpu.VMEM((NX, CHUNK * BE, PX), jnp.bfloat16),
             pltpu.VMEM((2, BE, PX, PX), jnp.bfloat16),
             pltpu.VMEM((BE, CHUNK, PX), jnp.bfloat16),
             pltpu.VMEM((2, BE, CHUNK, PX), jnp.float32),
             pltpu.VMEM((NB, 128), jnp.float32),
-            pltpu.VMEM((NX * NY, 2, 4, BE, 128), jnp.int16),
-            *[pltpu.VMEM((NY, 2, 4, BE, 128), jnp.int16) for _ in range(NX)],
+            pltpu.VMEM((NX, 8, 2, 4, BE, 128), jnp.int16),
+            pltpu.VMEM((NX, 4, 2, 4, BE, 128), jnp.int16),
+            pltpu.VMEM((NX, 4, 2, 4, BE, 128), jnp.int16),
+            *[pltpu.VMEM((4, 2, 4, BE, 128), jnp.int16) for _ in range(NX)],
             pltpu.VMEM((NX, 2, 4, BE, 128), jnp.float32),
+            pltpu.SemaphoreType.DMA((6,)),
             pltpu.SemaphoreType.DMA((NX,)),
             pltpu.SemaphoreType.DMA((2,)),
-            pltpu.SemaphoreType.DMA((NX * NY,)),
-            pltpu.SemaphoreType.DMA((NX * NY,)),
+            pltpu.SemaphoreType.DMA((NX,)),
+            pltpu.SemaphoreType.DMA((NX,)),
+            pltpu.SemaphoreType.DMA((NX * 4,)),
+            pltpu.SemaphoreType.DMA((NX * 4,)),
             pltpu.SemaphoreType.DMA,
         ],
         compiler_params=pltpu.CompilerParams(
-            collective_id=0, has_side_effects=True, vmem_limit_bytes=40 * 2**20
+            collective_id=0, has_side_effects=True, vmem_limit_bytes=58 * 2**20
         ),
     )(order, color_gain, color_bias, ext_gain, ext_bias, cost, bricks.reshape(NB * BE, PX), table)
 

time: 46.1 us -> 38.9 us (0.84)
  the two profiles are of different devices: /device:TPU:450 before, /device:TPU:452 now
where the time goes in v2:
time: 38.9 us; the launch traced here: 38.7 us
  Pallas kernels  36 us (93%)
  local copies, waits for them, and re-layouts  1.47 us (4%)
  between operations  1.3 us (3%)
    pallas_call x1, Pallas kernels, shards(): pl.pallas_call(kernel, out_shape=jax.ShapeDtypeStruct((2, 4, 8, 256), jnp...  36 us
    unnamed x1, local copies, waits for them, and re-layouts  1.47 us

profile of v2, /device:TPU:452, one launch (start us, length us, event | category | flops | bytes accessed | tf_op | source)
XLA Modules:
  0.0 38.7 jit_solution(7266065043118469733)
XLA Ops:
  1.3 36.0 %shard_map.82 = f32[2,4,8,256]{3,2,1,0:T(8,128)} custom-call(s32[2,32]{1,0:T(2,128)} %order_hbm.1, f32[3]{0:T(128)} %color_gain_hbm.1, f32[3]{0:T(128)} %color_bias_hbm.1, f32[1]{0:T(128)S(6)} %copy.10.ext_gain_hbm, f32[1]{0:T(128)S(6)} %copy.11.ext_bias_hbm, s32[1,256]{1,0:T(1,128)} %cost_hbm.1, bf16[4096,256]{1,0:T(8,128)(2,1)} %bitcast.1, ...), custom_call_target="tpu_custom_call" | custom-call | tf_op jit(solution)/shard_map/pallas_call | solution.py:298
  37.3 1.5 %copy.12 = f32[2,4,8,256]{3,2,1,0:T(8,128)} copy(f32[2,4,8,256]{3,2,1,0:T(8,128)} %shard_map.82) | data formatting | bytes 131072

commit v3 on v2

v3 whole, which is shorter than its diff:
```python
import jax
import jax.numpy as jnp
import numpy as np
import ml_dtypes
from jax import lax
from jax.experimental import pallas as pl
from jax.experimental.pallas import tpu as pltpu
from jax.sharding import PartitionSpec as P

BE = 16
PX = BE * BE
NB = 256
NX = 4
NY = 8
CHUNK = NB // NX
SHEAR = (0.45, -0.3)
LOG2E = 1.4426950408889634
TOP = 65535.0
MESH = pl.DeviceIdType.MESH


def shear_table():
    cells = np.arange(PX)
    rows, cols = cells // BE, cells % BE
    out = np.zeros((2, BE, PX, PX), np.float32)
    for view in range(2):
        k = np.arange(BE, dtype=np.float32)[:, None]
        position = np.arange(BE, dtype=np.float32)[None, :] + np.float32(SHEAR[view]) * (
            k - np.float32((BE - 1) / 2.0)
        )
        anchor = np.floor(position)
        fraction = (position - anchor).astype(np.float32)
        low = (np.float32(1.0) - fraction).astype(ml_dtypes.bfloat16).astype(np.float32)
        high = fraction.astype(ml_dtypes.bfloat16).astype(np.float32)
        anchor = anchor.astype(np.int32)
        along = cols if view == 0 else rows
        for tap, weight in ((0, low), (1, high)):
            source = anchor[:, along] + tap
            inside = (source >= 0) & (source < BE)
            for s in range(BE):
                index = (rows * BE + source[s]) if view == 0 else (source[s] * BE + cols)
                ok = inside[s]
                out[view, s, index[ok], cells[ok]] += weight[s, along][ok]
    return out.astype(ml_dtypes.bfloat16)


def encode(value):
    root = jnp.exp2(0.25 * jnp.log2(jnp.maximum(value, 1e-30)))
    code = jnp.minimum(root * TOP + 0.5, TOP).astype(jnp.int32) - 32768
    return code.astype(jnp.int16)


def decode(code):
    root = (code.astype(jnp.float32) + 32768.0) * (1.0 / TOP)
    square = root * root
    return square * square


def swap_rows_and_groups(block):
    row = lax.broadcasted_iota(jnp.int32, (8, 128), 0)
    group = lax.broadcasted_iota(jnp.int32, (8, 128), 1) // 16
    for bit in (1, 2, 4):
        row_bit = (row & bit) != 0
        group_bit = (group & bit) != 0
        from_below = pltpu.roll(pltpu.roll(block, 8 - bit, 0), 16 * bit, 1)
        from_above = pltpu.roll(pltpu.roll(block, bit, 0), 128 - 16 * bit, 1)
        moved = jnp.where(row_bit, from_above, from_below)
        block = jnp.where(row_bit == group_bit, block, moved)
    return block


def kernel(
    order_hbm, color_gain_hbm, color_bias_hbm, ext_gain_hbm, ext_bias_hbm, cost_hbm, bricks, table_hbm, out,
    order, color_gain, color_bias, ext_gain, ext_bias, cost, raw, table, sliced, samples, offset, slab, other, pair_out, *rest,
):
    pair_in = (rest[:NX], rest[NX:2 * NX])
    (
        group, small_sem, raw_sem, table_sem, slab_send_sem, slab_recv_sem,
        pair_send_sem, pair_recv_sem, own_sem,
    ) = rest[2 * NX:]
    me = lax.axis_index("depth")
    x, y = me // NY, me % NY

    def chunk_copy(i):
        c = lax.rem(x + i + 1, NX)
        rows = pl.ds(pl.multiple_of(c * CHUNK * BE, CHUNK * BE), CHUNK * BE)
        return pltpu.make_async_copy(bricks.at[rows], raw.at[i], raw_sem.at[i])

    def table_copy(view):
        return pltpu.make_async_copy(table_hbm.at[view], table.at[view], table_sem.at[view])

    small = [
        pltpu.make_async_copy(source, target, small_sem.at[n])
        for n, (source, target) in enumerate((
            (cost_hbm, cost), (order_hbm, order), (ext_gain_hbm, ext_gain), (ext_bias_hbm, ext_bias),
            (color_gain_hbm, color_gain), (color_bias_hbm, color_bias),
        ))
    ]
    for copy in small:
        copy.start()
    chunk_copy(0).start()
    table_copy(0).start()
    table_copy(1).start()
    for i in range(1, NX):
        chunk_copy(i).start()

    odd = lax.rem(y, 2)
    way = 2 * odd - 1
    partner = x * NY + y - way

    def peer(i, t):
        return lax.rem(x + i, NX) * NY + lax.rem(y + way * t + NY, NY)

    barrier = pltpu.get_barrier_semaphore()

    def greet(device):
        pl.semaphore_signal(barrier, inc=1, device_id={"depth": device}, device_id_type=MESH)

    greet(partner)
    for i in range(NX):
        for t, step in enumerate((0, way, -2 * way, 3 * way)):
            if i or t:
                greet(lax.rem(x + NX - i, NX) * NY + lax.rem(y + step + NY, NY))

    for copy in small:
        copy.wait()

    r = lax.broadcasted_iota(jnp.int32, (NB, NB), 0)
    q = lax.broadcasted_iota(jnp.int32, (NB, NB), 1)
    diagonal = jnp.where(r == q, (cost[...] * 4).astype(jnp.float32), 0.0).astype(jnp.bfloat16)
    level = jnp.dot(diagonal, jnp.ones((NB, 128), jnp.bfloat16), preferred_element_type=jnp.float32)
    gain = ext_gain[0] * LOG2E
    bias = ext_bias[0] * LOG2E + float(np.log2(LOG2E))
    for k in range(BE):
        offset[k] = jnp.where(k < level, bias, -1e9)
    regroup = jnp.where(q == (r % BE) * BE + r // BE, 1.0, 0.0).astype(jnp.bfloat16)

    masks = [order[v, 0] for v in range(2)]
    turned = [jnp.where(order[v, 0] > order[v, 31], 15, 0) for v in range(2)]
    half_gain = [color_gain[c] * 0.5 for c in range(3)]
    half_bias = [color_bias[c] * 0.5 for c in range(3)]

    def to_partner(view, n):
        return pltpu.make_async_remote_copy(
            src_ref=slab.at[view, n, pl.ds(4, 4)], dst_ref=other.at[view, n],
            send_sem=slab_send_sem.at[view * NX + n], recv_sem=slab_recv_sem.at[view * NX + n],
            device_id={"depth": partner}, device_id_type=MESH,
        )

    def to_owner(view, n, t):
        sem = (view * NX + n) * 4 + t
        return pltpu.make_async_remote_copy(
            src_ref=pair_out.at[view, n, t], dst_ref=pair_in[view][n].at[t],
            send_sem=pair_send_sem.at[sem], recv_sem=pair_recv_sem.at[sem],
            device_id={"depth": peer(n + 1, t)}, device_id_type=MESH,
        )

    def own_copy(view):
        return pltpu.make_async_copy(
            pair_out.at[view, NX - 1, 0], pair_in[view][NX - 1].at[0], own_sem.at[view]
        )

    def regroup_chunk(i):
        chunk_copy(i).wait()
        for g in range(CHUNK // BE):
            lined = jnp.dot(
                regroup, raw[i, g * PX:(g + 1) * PX, :], preferred_element_type=jnp.float32
            ).astype(jnp.bfloat16)
            rows = pl.ds(pl.multiple_of(i * CHUNK + g * BE, BE), BE)
            for k in range(BE):
                sliced[k, rows, :] = lined[k * BE:(k + 1) * BE, :]

    def resample_rows(view, first, count):
        def resample(k, carry):
            mixed = jnp.dot(
                sliced[k, first:first + count], table[view, k], preferred_element_type=jnp.float32
            )
            for h in range(2):
                samples[view, k, h, first:first + count] = mixed[:, h * 128:(h + 1) * 128]
            return carry

        lax.fori_loop(0, BE, resample, 0, unroll=4)

    def shade_part(view, n, part):
        c = lax.rem(x + n + 1, NX)

        def shade(pair, carry):
            places = []
            for e in range(2):
                u = part * 4 + pair * 2 + e
                row = lax.rem(y + way * u + NY, NY)
                g, h = row // 2, lax.rem(row, 2)
                places.append((
                    u, h, pl.ds(pl.multiple_of(n * CHUNK + g * BE, BE), BE),
                    pl.ds(pl.multiple_of(c * CHUNK + g * BE, BE), BE),
                ))
            depth = jnp.zeros((2 * BE, 128), jnp.float32)
            clear = jnp.ones((2 * BE, 128), jnp.float32)
            tints = [jnp.zeros((2 * BE, 128), jnp.float32) for _ in range(3)]
            for k in range(BE):
                kk = jnp.bitwise_xor(k, turned[view])
                s = jnp.concatenate([samples[view, kk, h, rows, :] for _, h, rows, _ in places], axis=0)
                b = jnp.concatenate([offset[kk, rows, :] for _, _, _, rows in places], axis=0)
                depth = depth - jnp.exp2(s * gain + b)
                after = jnp.exp2(depth)
                weight = clear - after
                clear = after
                for ch in range(3):
                    tints[ch] = tints[ch] + weight * jnp.tanh(s * half_gain[ch] + half_bias[ch])
            opaque = 1.0 - clear
            values = [0.5 * (opaque + t) for t in tints] + [opaque]
            for ch in range(4):
                code = encode(values[ch])
                for e in range(2):
                    slab[view, n, places[e][0], ch] = code[e * BE:(e + 1) * BE]
            return carry

        lax.fori_loop(0, 2, shade, 0)

    def send_slab(view, n):
        shade_part(view, n, 1)
        to_partner(view, n).start()

    def composite_pair(view, n):
        first = (jnp.bitwise_xor(y, masks[view]) & 1) == 0
        to_partner(view, n).wait_recv()

        def one(t, carry):
            mine = [decode(slab[view, n, t, ch]) for ch in range(4)]
            theirs = [decode(other[view, n, 3 - t, ch]) for ch in range(4)]
            keep_mine = jnp.where(first, 1.0, 1.0 - theirs[3])
            keep_theirs = jnp.where(first, 1.0 - mine[3], 1.0)
            for ch in range(4):
                pair_out[view, n, t, ch] = encode(keep_mine * mine[ch] + keep_theirs * theirs[ch])
            return carry

        lax.fori_loop(0, 4, one, 0)

    def send_pairs(view, n):
        def go(t, carry):
            to_owner(view, n, t).start()
            return carry

        if n == NX - 1:
            own_copy(view).start()
        lax.fori_loop(1 if n == NX - 1 else 0, 4, go, 0)

    def finish_column(view, n):
        shade_part(view, n, 0)
        composite_pair(view, n)
        for step in range(NX):
            pl.when(n == step)(lambda step=step: send_pairs(view, step))

    def loop(start, body):
        def step(n, carry):
            body(n)
            return carry

        lax.fori_loop(start, NX, step, 0)

    regroup_chunk(0)
    table_copy(0).wait()
    resample_rows(0, 0, CHUNK)
    shade_part(0, 0, 1)
    pl.semaphore_wait(barrier, 4 * NX)
    to_partner(0, 0).start()
    loop(1, regroup_chunk)
    resample_rows(0, CHUNK, NB - CHUNK)
    loop(1, lambda n: send_slab(0, n))
    table_copy(1).wait()
    resample_rows(1, 0, NB)

    def both(n):
        send_slab(1, n)
        finish_column(0, n)

    loop(0, both)
    loop(0, lambda n: finish_column(1, n))

    for view in range(2):
        for n in range(NX):
            first = 0
            if n == NX - 1:
                own_copy(view).wait()
                first = 1

            def wait_in(t, carry):
                to_owner(view, n, t).wait_recv()
                return carry

            lax.fori_loop(first, 4, wait_in, 0)
            clear = jnp.ones((BE, 128), jnp.float32)
            total = [jnp.zeros((BE, 128), jnp.float32) for _ in range(4)]
            for rank in range(4):
                pair = jnp.bitwise_xor(rank, (masks[view] // 2) & 3)
                delta = (way * (pair - y // 2)) & 3
                t = jnp.bitwise_xor(delta, delta // 2)
                for ch in range(4):
                    total[ch] = total[ch] + clear * decode(pair_in[view][n][t, ch])
                clear = 1.0 - total[3]
            for ch in range(4):
                group[view, n, ch] = total[ch]

        clear = jnp.ones((BE, 128), jnp.float32)
        total = [jnp.zeros((BE, 128), jnp.float32) for _ in range(4)]
        for rank in range(NX):
            source = jnp.bitwise_xor(rank, masks[view] // NY)
            n = (x - source - 1) & (NX - 1)
            for ch in range(4):
                total[ch] = total[ch] + clear * group[view, n, ch]
            clear = 1.0 - total[3]
        for ch in range(4):
            for h in range(2):
                out[view, ch, :, h * 128:(h + 1) * 128] = swap_rows_and_groups(total[ch][h * 8:(h + 1) * 8, :])

    for view in range(2):
        for n in range(NX):
            to_partner(view, n).wait_send()

            def wait_out(t, carry):
                to_owner(view, n, t).wait_send()
                return carry

            lax.fori_loop(1 if n == NX - 1 else 0, 4, wait_out, 0)


def shards(bricks, cost, order, color_gain, color_bias, ext_gain, ext_bias):
    table = jnp.asarray(shear_table())
    vmem = pl.BlockSpec(memory_space=pltpu.VMEM)
    anywhere = pl.BlockSpec(memory_space=pltpu.HBM)
    return pl.pallas_call(
        kernel,
        out_shape=jax.ShapeDtypeStruct((2, 4, 8, 256), jnp.float32),
        in_specs=[anywhere] * 8,
        out_specs=vmem,
        scratch_shapes=[
            pltpu.SMEM((2, 32), jnp.int32),
            pltpu.SMEM((3,), jnp.float32),
            pltpu.SMEM((3,), jnp.float32),
            pltpu.SMEM((1,), jnp.float32),
            pltpu.SMEM((1,), jnp.float32),
            pltpu.VMEM((1, NB), jnp.int32),
            pltpu.VMEM((NX, CHUNK * BE, PX), jnp.bfloat16),
            pltpu.VMEM((2, BE, PX, PX), jnp.bfloat16),
            pltpu.VMEM((BE, NB, PX), jnp.bfloat16),
            pltpu.VMEM((2, BE, 2, NB, 128), jnp.float32),
            pltpu.VMEM((BE, NB, 128), jnp.float32),
            pltpu.VMEM((2, NX, 8, 4, BE, 128), jnp.int16),
            pltpu.VMEM((2, NX, 4, 4, BE, 128), jnp.int16),
            pltpu.VMEM((2, NX, 4, 4, BE, 128), jnp.int16),
            *[pltpu.VMEM((4, 4, BE, 128), jnp.int16) for _ in range(2 * NX)],
            pltpu.VMEM((2, NX, 4, BE, 128), jnp.float32),
            pltpu.SemaphoreType.DMA((6,)),
            pltpu.SemaphoreType.DMA((NX,)),
            pltpu.SemaphoreType.DMA((2,)),
            pltpu.SemaphoreType.DMA((NX * 2,)),
            pltpu.SemaphoreType.DMA((NX * 2,)),
            pltpu.SemaphoreType.DMA((2 * NX * 4,)),
            pltpu.SemaphoreType.DMA((2 * NX * 4,)),
            pltpu.SemaphoreType.DMA((2,)),
        ],
        compiler_params=pltpu.CompilerParams(
            collective_id=0, has_side_effects=True, vmem_limit_bytes=58 * 2**20
        ),
    )(order, color_gain, color_bias, ext_gain, ext_bias, cost, bricks.reshape(NB * BE, PX), table)


def solution(mesh):
    in_specs = (P("depth", "image", None, None), P("depth", "image"), P(), P(), P(), P(), P())
    out_specs = P(None, None, "depth", "image")
    return jax.shard_map(shards, mesh=mesh, in_specs=in_specs, out_specs=out_specs, check_vma=False)
```

time: 38.9 us -> 35.5 us (0.913)
  the two profiles are of different devices: /device:TPU:452 before, /device:TPU:8 now
where the time goes in v3:
time: 35.5 us; the launch traced here: 35.3 us
  Pallas kernels  32.6 us (92%)
  local copies, waits for them, and re-layouts  1.47 us (4%)
  between operations  1.3 us (4%)
    pallas_call x1, Pallas kernels, shards(): pl.pallas_call(kernel, out_shape=jax.ShapeDtypeStruct((2, 4, 8, 256), jnp...  32.6 us
    unnamed x1, local copies, waits for them, and re-layouts  1.47 us

profile of v3, /device:TPU:8, one launch (start us, length us, event | category | flops | bytes accessed | tf_op | source)
XLA Modules:
  0.0 35.3 jit_solution(11057586196029209769)
XLA Ops:
  1.3 32.6 %shard_map.82 = f32[2,4,8,256]{3,2,1,0:T(8,128)} custom-call(s32[2,32]{1,0:T(2,128)} %order_hbm.1, f32[3]{0:T(128)} %color_gain_hbm.1, f32[3]{0:T(128)} %color_bias_hbm.1, f32[1]{0:T(128)S(6)} %copy.10.ext_gain_hbm, f32[1]{0:T(128)S(6)} %copy.11.ext_bias_hbm, s32[1,256]{1,0:T(1,128)} %cost_hbm.1, bf16[4096,256]{1,0:T(8,128)(2,1)} %bitcast.1, ...), custom_call_target="tpu_custom_call" | custom-call | tf_op jit(solution)/shard_map/pallas_call | solution.py:331
  33.9 1.5 %copy.12 = f32[2,4,8,256]{3,2,1,0:T(8,128)} copy(f32[2,4,8,256]{3,2,1,0:T(8,128)} %shard_map.82) | data formatting | bytes 131072

commit v4 on v3

--- a/solution.py
+++ b/solution.py
@@ -70,8 +70,8 @@
 
 
 def kernel(
-    order_hbm, color_gain_hbm, color_bias_hbm, ext_gain_hbm, ext_bias_hbm, cost_hbm, bricks, table_hbm, out,
-    order, color_gain, color_bias, ext_gain, ext_bias, cost, raw, table, sliced, samples, offset, slab, other, pair_out, *rest,
+    order_hbm, color_gain_hbm, color_bias_hbm, ext_gain_hbm, ext_bias_hbm, cost_hbm, bricks, cell_hbm, table_hbm, out,
+    order, color_gain, color_bias, ext_gain, ext_bias, cost, raw, cell, table, sliced, samples, offset, slab, other, pair_out, *rest,
 ):
     pair_in = (rest[:NX], rest[NX:2 * NX])
     (
@@ -86,8 +86,8 @@
         rows = pl.ds(pl.multiple_of(c * CHUNK * BE, CHUNK * BE), CHUNK * BE)
         return pltpu.make_async_copy(bricks.at[rows], raw.at[i], raw_sem.at[i])
 
-    def table_copy(view):
-        return pltpu.make_async_copy(table_hbm.at[view], table.at[view], table_sem.at[view])
+    cell_copy = pltpu.make_async_copy(cell_hbm, cell, table_sem.at[0])
+    table_copy = pltpu.make_async_copy(table_hbm, table.at[1], table_sem.at[1])
 
     small = [
         pltpu.make_async_copy(source, target, small_sem.at[n])
@@ -98,11 +98,10 @@
     ]
     for copy in small:
         copy.start()
-    chunk_copy(0).start()
-    table_copy(0).start()
-    table_copy(1).start()
-    for i in range(1, NX):
+    cell_copy.start()
+    for i in range(NX):
         chunk_copy(i).start()
+    table_copy.start()
 
     odd = lax.rem(y, 2)
     way = 2 * odd - 1
@@ -179,7 +178,7 @@
                 samples[view, k, h, first:first + count] = mixed[:, h * 128:(h + 1) * 128]
             return carry
 
-        lax.fori_loop(0, BE, resample, 0, unroll=4)
+        lax.fori_loop(0, BE, resample, 0, unroll=16)
 
     def shade_part(view, n, part):
         c = lax.rem(x + n + 1, NX)
@@ -258,8 +257,21 @@
 
         lax.fori_loop(start, NX, step, 0)
 
+    group_of = lax.broadcasted_iota(jnp.int32, (BE, 128), 1) // BE
+    keep = [jnp.where(group_of == i, 1.0, 0.0).astype(jnp.bfloat16) for i in range(8)]
+    nothing = jnp.zeros((BE, 128), jnp.bfloat16)
+    cell_copy.wait()
+
+    def spread(k, carry):
+        for i in range(BE):
+            for j in range(2):
+                table[0, k, i * BE:(i + 1) * BE, j * 128:(j + 1) * 128] = (
+                    cell[k] * keep[i % 8] if i // 8 == j else nothing
+                )
+        return carry
+
+    lax.fori_loop(0, BE, spread, 0)
     regroup_chunk(0)
-    table_copy(0).wait()
     resample_rows(0, 0, CHUNK)
     shade_part(0, 0, 1)
     pl.semaphore_wait(barrier, 4 * NX)
@@ -267,7 +279,7 @@
     loop(1, regroup_chunk)
     resample_rows(0, CHUNK, NB - CHUNK)
     loop(1, lambda n: send_slab(0, n))
-    table_copy(1).wait()
+    table_copy.wait()
     resample_rows(1, 0, NB)
 
     def both(n):
@@ -325,13 +337,19 @@
 
 
 def shards(bricks, cost, order, color_gain, color_bias, ext_gain, ext_bias):
-    table = jnp.asarray(shear_table())
+    tables = shear_table()
+    cell = jnp.asarray(np.tile(tables[0, :, :BE, :BE], (1, 1, 8)))
+    table = jnp.asarray(tables[1])
     vmem = pl.BlockSpec(memory_space=pltpu.VMEM)
+
+    def hbm(array):
+        return pltpu.with_memory_space_constraint(array, pltpu.HBM)
+
     anywhere = pl.BlockSpec(memory_space=pltpu.HBM)
     return pl.pallas_call(
         kernel,
         out_shape=jax.ShapeDtypeStruct((2, 4, 8, 256), jnp.float32),
-        in_specs=[anywhere] * 8,
+        in_specs=[anywhere] * 9,
         out_specs=vmem,
         scratch_shapes=[
             pltpu.SMEM((2, 32), jnp.int32),
@@ -341,6 +359,7 @@
             pltpu.SMEM((1,), jnp.float32),
             pltpu.VMEM((1, NB), jnp.int32),
             pltpu.VMEM((NX, CHUNK * BE, PX), jnp.bfloat16),
+            pltpu.VMEM((BE, BE, 128), jnp.bfloat16),
             pltpu.VMEM((2, BE, PX, PX), jnp.bfloat16),
             pltpu.VMEM((BE, NB, PX), jnp.bfloat16),
             pltpu.VMEM((2, BE, 2, NB, 128), jnp.float32),
@@ -360,9 +379,9 @@
             pltpu.SemaphoreType.DMA((2,)),
         ],
         compiler_params=pltpu.CompilerParams(
-            collective_id=0, has_side_effects=True, vmem_limit_bytes=58 * 2**20
+            collective_id=0, has_side_effects=True, vmem_limit_bytes=48 * 2**20
         ),
-    )(order, color_gain, color_bias, ext_gain, ext_bias, cost, bricks.reshape(NB * BE, PX), table)
+    )(hbm(order), hbm(color_gain), hbm(color_bias), ext_gain, ext_bias, hbm(cost), hbm(bricks.reshape(NB * BE, PX)), hbm(cell), hbm(table))
 
 
 def solution(mesh):

time: 35.5 us -> 33.2 us (0.935)
  Pallas kernels: 32.6 us -> 31.2 us
  local copies, waits for them, and re-layouts: 1.47 us -> 0.63 us
    pallas_call x1, Pallas kernels: 32.6 us -> 31.2 us  [shards(): pl.pallas_call(kernel, out_shape=jax.ShapeDtypeStruct((2, 4, 8, 256), jnp...]
    unnamed x1, local copies, waits for them, and re-layouts: 1.47 us -> 0.63 us
where the time goes in v4:
time: 33.2 us; the launch traced here: 33.1 us
  Pallas kernels  31.2 us (94%)
  between operations  1.3 us (4%)
  local copies, waits for them, and re-layouts  0.63 us (2%)
    pallas_call x1, Pallas kernels, shards(): pl.pallas_call(kernel, out_shape=jax.ShapeDtypeStruct((2, 4, 8, 256), jnp...  31.2 us

profile of v4, /device:TPU:8, one launch (start us, length us, event | category | flops | bytes accessed | tf_op | source)
XLA Modules:
  0.0 33.1 jit_solution(17005933164152739359)
XLA Ops:
  1.3 31.2 %shard_map.91 = f32[2,4,8,256]{3,2,1,0:T(8,128)S(1)} custom-call(s32[2,32]{1,0:T(2,128)} %order_hbm.1, f32[3]{0:T(128)} %color_gain_hbm.1, f32[3]{0:T(128)} %color_bias_hbm.1, f32[1]{0:T(128)S(6)} %copy.11.ext_gain_hbm, f32[1]{0:T(128)S(6)} %copy.12.ext_bias_hbm, s32[1,256]{1,0:T(1,128)} %cost_hbm.1, bf16[4096,256]{1,0:T(8,128)(2,1)} %bitcast.1, ...), custom_call_target="tpu_custom_call" | custom-call | tf_op jit(solution)/shard_map/pallas_call | solution.py:349
  32.5 0.6 %copy.13 = f32[2,4,8,256]{3,2,1,0:T(8,128)} copy(f32[2,4,8,256]{3,2,1,0:T(8,128)S(1)} %shard_map.91) | data formatting | bytes 131072

commit v5 on v4

--- a/solution.py
+++ b/solution.py
@@ -71,11 +71,11 @@
 
 def kernel(
     order_hbm, color_gain_hbm, color_bias_hbm, ext_gain_hbm, ext_bias_hbm, cost_hbm, bricks, cell_hbm, table_hbm, out,
-    order, color_gain, color_bias, ext_gain, ext_bias, cost, raw, cell, table, sliced, samples, offset, slab, other, pair_out, *rest,
+    order, color_gain, color_bias, ext_gain, ext_bias, cost, raw, cell, near, table, sliced, samples, offset, slab, other, pair_out, *rest,
 ):
     pair_in = (rest[:NX], rest[NX:2 * NX])
     (
-        group, small_sem, raw_sem, table_sem, slab_send_sem, slab_recv_sem,
+        staged, group, small_sem, raw_sem, table_sem, slab_send_sem, slab_recv_sem,
         pair_send_sem, pair_recv_sem, own_sem,
     ) = rest[2 * NX:]
     me = lax.axis_index("depth")
@@ -87,7 +87,7 @@
         return pltpu.make_async_copy(bricks.at[rows], raw.at[i], raw_sem.at[i])
 
     cell_copy = pltpu.make_async_copy(cell_hbm, cell, table_sem.at[0])
-    table_copy = pltpu.make_async_copy(table_hbm, table.at[1], table_sem.at[1])
+    table_copy = pltpu.make_async_copy(table_hbm, table, table_sem.at[1])
 
     small = [
         pltpu.make_async_copy(source, target, small_sem.at[n])
@@ -115,10 +115,9 @@
     def greet(device):
         pl.semaphore_signal(barrier, inc=1, device_id={"depth": device}, device_id_type=MESH)
 
-    greet(partner)
     for i in range(NX):
-        for t, step in enumerate((0, way, -2 * way, 3 * way)):
-            if i or t:
+        for step in (0, -way, way, 2 * way, -2 * way, 3 * way):
+            if i or not isinstance(step, int):
                 greet(lax.rem(x + NX - i, NX) * NY + lax.rem(y + step + NY, NY))
 
     for copy in small:
@@ -139,24 +138,27 @@
     half_gain = [color_gain[c] * 0.5 for c in range(3)]
     half_bias = [color_bias[c] * 0.5 for c in range(3)]
 
+    slots = {0: 0, 7: 1, 1: 2, 6: 3, 2: 4, 3: 5}
+
     def to_partner(view, n):
         return pltpu.make_async_remote_copy(
-            src_ref=slab.at[view, n, pl.ds(4, 4)], dst_ref=other.at[view, n],
+            src_ref=slab.at[view, n, pl.ds(4, 2)], dst_ref=other.at[view, n],
             send_sem=slab_send_sem.at[view * NX + n], recv_sem=slab_recv_sem.at[view * NX + n],
             device_id={"depth": partner}, device_id_type=MESH,
         )
 
-    def to_owner(view, n, t):
-        sem = (view * NX + n) * 4 + t
+    def to_owner(view, n, u):
+        sem = (view * NX + n) * 6 + slots[u]
         return pltpu.make_async_remote_copy(
-            src_ref=pair_out.at[view, n, t], dst_ref=pair_in[view][n].at[t],
+            src_ref=pair_out.at[view, n, u - 2] if u in (2, 3) else slab.at[view, n, u],
+            dst_ref=pair_in[view][n].at[slots[u]],
             send_sem=pair_send_sem.at[sem], recv_sem=pair_recv_sem.at[sem],
-            device_id={"depth": peer(n + 1, t)}, device_id_type=MESH,
+            device_id={"depth": peer(n + 1, u)}, device_id_type=MESH,
         )
 
     def own_copy(view):
         return pltpu.make_async_copy(
-            pair_out.at[view, NX - 1, 0], pair_in[view][NX - 1].at[0], own_sem.at[view]
+            slab.at[view, NX - 1, 0], pair_in[view][NX - 1].at[0], own_sem.at[view]
         )
 
     def regroup_chunk(i):
@@ -167,26 +169,35 @@
             ).astype(jnp.bfloat16)
             rows = pl.ds(pl.multiple_of(i * CHUNK + g * BE, BE), BE)
             for k in range(BE):
-                sliced[k, rows, :] = lined[k * BE:(k + 1) * BE, :]
+                for h in range(2):
+                    sliced[k, h, rows, :] = lined[k * BE:(k + 1) * BE, h * 128:(h + 1) * 128]
 
     def resample_rows(view, first, count):
         def resample(k, carry):
-            mixed = jnp.dot(
-                sliced[k, first:first + count], table[view, k], preferred_element_type=jnp.float32
-            )
+            halves = [sliced[k, h, first:first + count] for h in range(2)]
+            if view == 0:
+                mixed = jnp.dot(
+                    jnp.concatenate(halves, axis=0), near[k], preferred_element_type=jnp.float32
+                )
+                mixed = [mixed[:count], mixed[count:]]
+            else:
+                mixed = jnp.dot(
+                    jnp.concatenate(halves, axis=1), table[k], preferred_element_type=jnp.float32
+                )
+                mixed = [mixed[:, :128], mixed[:, 128:]]
             for h in range(2):
-                samples[view, k, h, first:first + count] = mixed[:, h * 128:(h + 1) * 128]
+                samples[view, k, h, first:first + count] = mixed[h]
             return carry
 
         lax.fori_loop(0, BE, resample, 0, unroll=16)
 
-    def shade_part(view, n, part):
+    def shade_part(view, n, first, end):
         c = lax.rem(x + n + 1, NX)
 
         def shade(pair, carry):
             places = []
             for e in range(2):
-                u = part * 4 + pair * 2 + e
+                u = pair * 2 + e
                 row = lax.rem(y + way * u + NY, NY)
                 g, h = row // 2, lax.rem(row, 2)
                 places.append((
@@ -214,41 +225,52 @@
                     slab[view, n, places[e][0], ch] = code[e * BE:(e + 1) * BE]
             return carry
 
-        lax.fori_loop(0, 2, shade, 0)
+        lax.fori_loop(first, end, shade, 0)
+
+    def over(a, b, first):
+        keep_a = jnp.where(first, 1.0, 1.0 - b[3])
+        keep_b = jnp.where(first, 1.0 - a[3], 1.0)
+        return [keep_a * a[ch] + keep_b * b[ch] for ch in range(4)]
+
+    def mine_first(view):
+        return (jnp.bitwise_xor(y, masks[view]) & 1) == 0
+
+    def send_direct(view, n, us):
+        for step in range(NX):
+
+            def go(step=step):
+                for u in us:
+                    if u == 0 and step == NX - 1:
+                        own_copy(view).start()
+                    else:
+                        to_owner(view, step, u).start()
+
+            if isinstance(n, int):
+                if n == step:
+                    go()
+            else:
+                pl.when(n == step)(go)
 
     def send_slab(view, n):
-        shade_part(view, n, 1)
+        shade_part(view, n, 2, 4)
+        if isinstance(n, int) and n == 0:
+            pl.semaphore_wait(barrier, 6 * NX - 1)
         to_partner(view, n).start()
-
-    def composite_pair(view, n):
-        first = (jnp.bitwise_xor(y, masks[view]) & 1) == 0
+        send_direct(view, n, (7, 6))
+
+    def finish_column(view, n):
+        shade_part(view, n, 0, 2)
         to_partner(view, n).wait_recv()
 
-        def one(t, carry):
-            mine = [decode(slab[view, n, t, ch]) for ch in range(4)]
-            theirs = [decode(other[view, n, 3 - t, ch]) for ch in range(4)]
-            keep_mine = jnp.where(first, 1.0, 1.0 - theirs[3])
-            keep_theirs = jnp.where(first, 1.0 - mine[3], 1.0)
-            for ch in range(4):
-                pair_out[view, n, t, ch] = encode(keep_mine * mine[ch] + keep_theirs * theirs[ch])
+        def one(e, carry):
+            mine = [decode(slab[view, n, 2 + e, ch]) for ch in range(4)]
+            theirs = [decode(other[view, n, 1 - e, ch]) for ch in range(4)]
+            for ch, value in enumerate(over(mine, theirs, mine_first(view))):
+                pair_out[view, n, e, ch] = encode(value)
             return carry
 
-        lax.fori_loop(0, 4, one, 0)
-
-    def send_pairs(view, n):
-        def go(t, carry):
-            to_owner(view, n, t).start()
-            return carry
-
-        if n == NX - 1:
-            own_copy(view).start()
-        lax.fori_loop(1 if n == NX - 1 else 0, 4, go, 0)
-
-    def finish_column(view, n):
-        shade_part(view, n, 0)
-        composite_pair(view, n)
-        for step in range(NX):
-            pl.when(n == step)(lambda step=step: send_pairs(view, step))
+        lax.fori_loop(0, 2, one, 0)
+        send_direct(view, n, (3, 2, 1, 0))
 
     def loop(start, body):
         def step(n, carry):
@@ -259,23 +281,17 @@
 
     group_of = lax.broadcasted_iota(jnp.int32, (BE, 128), 1) // BE
     keep = [jnp.where(group_of == i, 1.0, 0.0).astype(jnp.bfloat16) for i in range(8)]
-    nothing = jnp.zeros((BE, 128), jnp.bfloat16)
     cell_copy.wait()
 
     def spread(k, carry):
-        for i in range(BE):
-            for j in range(2):
-                table[0, k, i * BE:(i + 1) * BE, j * 128:(j + 1) * 128] = (
-                    cell[k] * keep[i % 8] if i // 8 == j else nothing
-                )
+        for i in range(8):
+            near[k, i * BE:(i + 1) * BE, :] = cell[k] * keep[i]
         return carry
 
     lax.fori_loop(0, BE, spread, 0)
     regroup_chunk(0)
     resample_rows(0, 0, CHUNK)
-    shade_part(0, 0, 1)
-    pl.semaphore_wait(barrier, 4 * NX)
-    to_partner(0, 0).start()
+    send_slab(0, 0)
     loop(1, regroup_chunk)
     resample_rows(0, CHUNK, NB - CHUNK)
     loop(1, lambda n: send_slab(0, n))
@@ -283,24 +299,33 @@
     resample_rows(1, 0, NB)
 
     def both(n):
-        send_slab(1, n)
+        shade_part(1, n, 2, 3)
+        to_partner(1, n).start()
         finish_column(0, n)
 
     loop(0, both)
-    loop(0, lambda n: finish_column(1, n))
+
+    def last(n):
+        finish_column(1, n)
+        shade_part(1, n, 3, 4)
+        send_direct(1, n, (7, 6))
+
+    loop(0, last)
 
     for view in range(2):
         for n in range(NX):
-            first = 0
-            if n == NX - 1:
-                own_copy(view).wait()
-                first = 1
-
-            def wait_in(t, carry):
-                to_owner(view, n, t).wait_recv()
-                return carry
-
-            lax.fori_loop(first, 4, wait_in, 0)
+            for u in slots:
+                if u == 0 and n == NX - 1:
+                    own_copy(view).wait()
+                else:
+                    to_owner(view, n, u).wait_recv()
+            raw_slabs = [[decode(pair_in[view][n][e, ch]) for ch in range(4)] for e in range(4)]
+            first = mine_first(view)
+            pairs = [over(raw_slabs[0], raw_slabs[1], first), over(raw_slabs[3], raw_slabs[2], first)]
+            pairs += [[decode(pair_in[view][n][e, ch]) for ch in range(4)] for e in (4, 5)]
+            for t in range(4):
+                for ch in range(4):
+                    staged[t, ch] = pairs[t][ch]
             clear = jnp.ones((BE, 128), jnp.float32)
             total = [jnp.zeros((BE, 128), jnp.float32) for _ in range(4)]
             for rank in range(4):
@@ -308,7 +333,7 @@
                 delta = (way * (pair - y // 2)) & 3
                 t = jnp.bitwise_xor(delta, delta // 2)
                 for ch in range(4):
-                    total[ch] = total[ch] + clear * decode(pair_in[view][n][t, ch])
+                    total[ch] = total[ch] + clear * staged[t, ch]
                 clear = 1.0 - total[3]
             for ch in range(4):
                 group[view, n, ch] = total[ch]
@@ -328,12 +353,9 @@
     for view in range(2):
         for n in range(NX):
             to_partner(view, n).wait_send()
-
-            def wait_out(t, carry):
-                to_owner(view, n, t).wait_send()
-                return carry
-
-            lax.fori_loop(1 if n == NX - 1 else 0, 4, wait_out, 0)
+            for u in slots:
+                if u or n < NX - 1:
+                    to_owner(view, n, u).wait_send()
 
 
 def shards(bricks, cost, order, color_gain, color_bias, ext_gain, ext_bias):
@@ -360,22 +382,24 @@
             pltpu.VMEM((1, NB), jnp.int32),
             pltpu.VMEM((NX, CHUNK * BE, PX), jnp.bfloat16),
             pltpu.VMEM((BE, BE, 128), jnp.bfloat16),
-            pltpu.VMEM((2, BE, PX, PX), jnp.bfloat16),
-            pltpu.VMEM((BE, NB, PX), jnp.bfloat16),
+            pltpu.VMEM((BE, 128, 128), jnp.bfloat16),
+            pltpu.VMEM((BE, PX, PX), jnp.bfloat16),
+            pltpu.VMEM((BE, 2, NB, 128), jnp.bfloat16),
             pltpu.VMEM((2, BE, 2, NB, 128), jnp.float32),
             pltpu.VMEM((BE, NB, 128), jnp.float32),
             pltpu.VMEM((2, NX, 8, 4, BE, 128), jnp.int16),
-            pltpu.VMEM((2, NX, 4, 4, BE, 128), jnp.int16),
-            pltpu.VMEM((2, NX, 4, 4, BE, 128), jnp.int16),
-            *[pltpu.VMEM((4, 4, BE, 128), jnp.int16) for _ in range(2 * NX)],
+            pltpu.VMEM((2, NX, 2, 4, BE, 128), jnp.int16),
+            pltpu.VMEM((2, NX, 2, 4, BE, 128), jnp.int16),
+            *[pltpu.VMEM((6, 4, BE, 128), jnp.int16) for _ in range(2 * NX)],
+            pltpu.VMEM((4, 4, BE, 128), jnp.float32),
             pltpu.VMEM((2, NX, 4, BE, 128), jnp.float32),
             pltpu.SemaphoreType.DMA((6,)),
             pltpu.SemaphoreType.DMA((NX,)),
             pltpu.SemaphoreType.DMA((2,)),
             pltpu.SemaphoreType.DMA((NX * 2,)),
             pltpu.SemaphoreType.DMA((NX * 2,)),
-            pltpu.SemaphoreType.DMA((2 * NX * 4,)),
-            pltpu.SemaphoreType.DMA((2 * NX * 4,)),
+            pltpu.SemaphoreType.DMA((2 * NX * 6,)),
+            pltpu.SemaphoreType.DMA((2 * NX * 6,)),
             pltpu.SemaphoreType.DMA((2,)),
         ],
         compiler_params=pltpu.CompilerParams(

time: 33.2 us -> 32.4 us (0.976)
  Pallas kernels: 31.2 us -> 30.3 us
    pallas_call x1, Pallas kernels: 31.2 us -> 30.3 us  [shards(): pl.pallas_call(kernel, out_shape=jax.ShapeDtypeStruct((2, 4, 8, 256), jnp...]
where the time goes in v5:
time: 32.4 us; the launch traced here: 32.2 us
  Pallas kernels  30.3 us (94%)
  between operations  1.3 us (4%)
  local copies, waits for them, and re-layouts  0.63 us (2%)
    pallas_call x1, Pallas kernels, shards(): pl.pallas_call(kernel, out_shape=jax.ShapeDtypeStruct((2, 4, 8, 256), jnp...  30.3 us

profile of v5, /device:TPU:8, one launch (start us, length us, event | category | flops | bytes accessed | tf_op | source)
XLA Modules:
  0.0 32.2 jit_solution(16709316730954118214)
XLA Ops:
  1.3 30.3 %shard_map.91 = f32[2,4,8,256]{3,2,1,0:T(8,128)S(1)} custom-call(s32[2,32]{1,0:T(2,128)} %order_hbm.1, f32[3]{0:T(128)} %color_gain_hbm.1, f32[3]{0:T(128)} %color_bias_hbm.1, f32[1]{0:T(128)S(6)} %copy.11.ext_gain_hbm, f32[1]{0:T(128)S(6)} %copy.12.ext_bias_hbm, s32[1,256]{1,0:T(1,128)} %cost_hbm.1, bf16[4096,256]{1,0:T(8,128)(2,1)} %bitcast.1, ...), custom_call_target="tpu_custom_call" | custom-call | tf_op jit(solution)/shard_map/pallas_call | solution.py:371
  31.6 0.6 %copy.13 = f32[2,4,8,256]{3,2,1,0:T(8,128)} copy(f32[2,4,8,256]{3,2,1,0:T(8,128)S(1)} %shard_map.91) | data formatting | bytes 131072

commit v6 on v5

--- a/solution.py
+++ b/solution.py
@@ -122,6 +122,8 @@
 
     for copy in small:
         copy.wait()
+    cell_copy.wait()
+    chunk_copy(0).wait()
 
     r = lax.broadcasted_iota(jnp.int32, (NB, NB), 0)
     q = lax.broadcasted_iota(jnp.int32, (NB, NB), 1)
@@ -129,12 +131,16 @@
     level = jnp.dot(diagonal, jnp.ones((NB, 128), jnp.bfloat16), preferred_element_type=jnp.float32)
     gain = ext_gain[0] * LOG2E
     bias = ext_bias[0] * LOG2E + float(np.log2(LOG2E))
-    for k in range(BE):
-        offset[k] = jnp.where(k < level, bias, -1e9)
     regroup = jnp.where(q == (r % BE) * BE + r // BE, 1.0, 0.0).astype(jnp.bfloat16)
 
     masks = [order[v, 0] for v in range(2)]
     turned = [jnp.where(order[v, 0] > order[v, 31], 15, 0) for v in range(2)]
+
+    def set_offset(view):
+        for k in range(BE):
+            kk = jnp.bitwise_xor(k, turned[view]).astype(jnp.float32)
+            offset[view, k] = jnp.where(kk < level, bias, -1e9)
+
     half_gain = [color_gain[c] * 0.5 for c in range(3)]
     half_bias = [color_bias[c] * 0.5 for c in range(3)]
 
@@ -162,7 +168,8 @@
         )
 
     def regroup_chunk(i):
-        chunk_copy(i).wait()
+        if not isinstance(i, int):
+            chunk_copy(i).wait()
         for g in range(CHUNK // BE):
             lined = jnp.dot(
                 regroup, raw[i, g * PX:(g + 1) * PX, :], preferred_element_type=jnp.float32
@@ -174,15 +181,16 @@
 
     def resample_rows(view, first, count):
         def resample(k, carry):
-            halves = [sliced[k, h, first:first + count] for h in range(2)]
+            kk = jnp.bitwise_xor(k, turned[view])
+            halves = [sliced[kk, h, first:first + count] for h in range(2)]
             if view == 0:
                 mixed = jnp.dot(
-                    jnp.concatenate(halves, axis=0), near[k], preferred_element_type=jnp.float32
+                    jnp.concatenate(halves, axis=0), near[kk], preferred_element_type=jnp.float32
                 )
                 mixed = [mixed[:count], mixed[count:]]
             else:
                 mixed = jnp.dot(
-                    jnp.concatenate(halves, axis=1), table[k], preferred_element_type=jnp.float32
+                    jnp.concatenate(halves, axis=1), table[kk], preferred_element_type=jnp.float32
                 )
                 mixed = [mixed[:, :128], mixed[:, 128:]]
             for h in range(2):
@@ -208,9 +216,8 @@
             clear = jnp.ones((2 * BE, 128), jnp.float32)
             tints = [jnp.zeros((2 * BE, 128), jnp.float32) for _ in range(3)]
             for k in range(BE):
-                kk = jnp.bitwise_xor(k, turned[view])
-                s = jnp.concatenate([samples[view, kk, h, rows, :] for _, h, rows, _ in places], axis=0)
-                b = jnp.concatenate([offset[kk, rows, :] for _, _, _, rows in places], axis=0)
+                s = jnp.concatenate([samples[view, k, h, rows, :] for _, h, rows, _ in places], axis=0)
+                b = jnp.concatenate([offset[view, k, rows, :] for _, _, _, rows in places], axis=0)
                 depth = depth - jnp.exp2(s * gain + b)
                 after = jnp.exp2(depth)
                 weight = clear - after
@@ -253,13 +260,11 @@
 
     def send_slab(view, n):
         shade_part(view, n, 2, 4)
-        if isinstance(n, int) and n == 0:
-            pl.semaphore_wait(barrier, 6 * NX - 1)
         to_partner(view, n).start()
         send_direct(view, n, (7, 6))
 
     def finish_column(view, n):
-        shade_part(view, n, 0, 2)
+        shade_part(view, n, 1, 2)
         to_partner(view, n).wait_recv()
 
         def one(e, carry):
@@ -270,7 +275,9 @@
             return carry
 
         lax.fori_loop(0, 2, one, 0)
-        send_direct(view, n, (3, 2, 1, 0))
+        send_direct(view, n, (3, 2))
+        shade_part(view, n, 0, 1)
+        send_direct(view, n, (1, 0))
 
     def loop(start, body):
         def step(n, carry):
@@ -281,20 +288,30 @@
 
     group_of = lax.broadcasted_iota(jnp.int32, (BE, 128), 1) // BE
     keep = [jnp.where(group_of == i, 1.0, 0.0).astype(jnp.bfloat16) for i in range(8)]
-    cell_copy.wait()
 
     def spread(k, carry):
         for i in range(8):
             near[k, i * BE:(i + 1) * BE, :] = cell[k] * keep[i]
         return carry
 
-    lax.fori_loop(0, BE, spread, 0)
+    lax.fori_loop(0, BE, spread, 0, unroll=16)
     regroup_chunk(0)
+    set_offset(0)
     resample_rows(0, 0, CHUNK)
-    send_slab(0, 0)
+    shade_part(0, 0, 2, 4)
+    set_offset(1)
     loop(1, regroup_chunk)
     resample_rows(0, CHUNK, NB - CHUNK)
-    loop(1, lambda n: send_slab(0, n))
+    pl.semaphore_wait(barrier, 6 * NX - 1)
+    to_partner(0, 0).start()
+    send_direct(0, 0, (7, 6))
+    def early(n):
+        shade_part(0, n, 2, 3)
+        to_partner(0, n).start()
+        shade_part(0, n, 3, 4)
+        send_direct(0, n, (7, 6))
+
+    loop(1, early)
     table_copy.wait()
     resample_rows(1, 0, NB)
 
@@ -386,7 +403,7 @@
             pltpu.VMEM((BE, PX, PX), jnp.bfloat16),
             pltpu.VMEM((BE, 2, NB, 128), jnp.bfloat16),
             pltpu.VMEM((2, BE, 2, NB, 128), jnp.float32),
-            pltpu.VMEM((BE, NB, 128), jnp.float32),
+            pltpu.VMEM((2, BE, NB, 128), jnp.float32),
             pltpu.VMEM((2, NX, 8, 4, BE, 128), jnp.int16),
             pltpu.VMEM((2, NX, 2, 4, BE, 128), jnp.int16),
             pltpu.VMEM((2, NX, 2, 4, BE, 128), jnp.int16),

time: 32.4 us -> 32.4 us (level)
  the two profiles are of different devices: /device:TPU:8 before, /device:TPU:128 now
where the time goes in v6:
time: 32.4 us; the launch traced here: 32.2 us
  Pallas kernels  30.3 us (94%)
  between operations  1.3 us (4%)
  local copies, waits for them, and re-layouts  0.63 us (2%)
    pallas_call x1, Pallas kernels, shards(): pl.pallas_call(kernel, out_shape=jax.ShapeDtypeStruct((2, 4, 8, 256), jnp...  30.3 us

profile of v6, /device:TPU:128, one launch (start us, length us, event | category | flops | bytes accessed | tf_op | source)
XLA Modules:
  0.0 32.2 jit_solution(10851552360696766684)
XLA Ops:
  1.3 30.3 %shard_map.91 = f32[2,4,8,256]{3,2,1,0:T(8,128)S(1)} custom-call(s32[2,32]{1,0:T(2,128)} %order_hbm.1, f32[3]{0:T(128)} %color_gain_hbm.1, f32[3]{0:T(128)} %color_bias_hbm.1, f32[1]{0:T(128)S(6)} %copy.11.ext_gain_hbm, f32[1]{0:T(128)S(6)} %copy.12.ext_bias_hbm, s32[1,256]{1,0:T(1,128)} %cost_hbm.1, bf16[4096,256]{1,0:T(8,128)(2,1)} %bitcast.1, ...), custom_call_target="tpu_custom_call" | custom-call | tf_op jit(solution)/shard_map/pallas_call | solution.py:388
  31.6 0.6 %copy.13 = f32[2,4,8,256]{3,2,1,0:T(8,128)} copy(f32[2,4,8,256]{3,2,1,0:T(8,128)S(1)} %shard_map.91) | data formatting | bytes 131072
